TPU v7x, 512 devices: a whole 4x8x8 slice. The times are simulated.
512 devices in a mesh: gx: 8 (over x, core), gy: 8 (over z), gz: 8 (over y).
Axes of the slice: x: 4, y: 8, z: 8, core: 2. Of those that a mesh axis runs over, the one named last changes fastest.
Arguments:
- phase_field: int32 [64, 128, 1024], P('gz', 'gx', 'gy'), may hold values 0 or 1
- thermal: float32 [64, 128, 1024], P('gz', 'gx', 'gy'), may hold values from 0.5 to 1.5
- velocity: float32 [3, 64, 128, 1024], P(None, 'gz', 'gx', 'gy'), may hold values from -6 to 6
- transfer_slope: float32 [8, 4], replicated, may hold values from -3 to 3
- transfer_offset: float32 [8, 4], replicated, may hold values from -1 to 1
- transfer_gain: float32 [8], replicated, may hold values from 0.5 to 4
Outputs:
- corrected: float32 [3, 64, 128, 1024], P(None, 'gz', 'gx', 'gy')
- images: float32 [8, 4, 128, 1024], P('gz', None, 'gx', 'gy')
All inputs are finite; a program needn't handle non-finite values. No bound on the sum of `phase_field` on one device may be relied on, other than what follows from the above.
Results may differ from a plain program's by a relative error of at most 0.0001.
Values sent between devices are 32-bit elements; how exact they have to be, the bound alone decides.
A program may use at most 64 MiB of HBM per device.

v0:
```python
import jax
import jax.numpy as jnp
from jax import lax
from jax.sharding import PartitionSpec as P

ITERS = 4


def padded_2(cells, sides, width):
    for axis, dim in sides:
        count = lax.axis_size(axis)
        ends = count - 1
        head = lax.slice_in_dim(cells, 0, width, axis=dim)
        tail = lax.slice_in_dim(cells, cells.shape[dim] - width, cells.shape[dim], axis=dim)
        cells = jnp.concatenate(
            [
                lax.ppermute(tail, axis, [(i, (i + 1) % count) for i in range(ends)]),
                cells,
                lax.ppermute(head, axis, [((i + 1) % count, i) for i in range(ends)]),
            ],
            axis=dim,
        )
    return cells


def prefix(value, axis, combine, identity):
    devices, here = (lax.axis_size(axis), lax.axis_index(axis))
    everything = lax.all_gather(value, axis)
    start = jnp.broadcast_to(jnp.asarray(identity, value.dtype), value.shape)

    def step(k, before):
        reached = k < here
        new = combine(before, everything[k])
        return jnp.where(reached, new, before)

    return lax.fori_loop(0, devices, step, start)


def inner(padded):
    return padded[1:-1, 1:-1, 1:-1]


def neighbours(padded, which):
    if which == 0:
        return (padded[:-2, 1:-1, 1:-1], padded[2:, 1:-1, 1:-1])
    if which == 1:
        return (padded[1:-1, :-2, 1:-1], padded[1:-1, 2:, 1:-1])
    return (padded[1:-1, 1:-1, :-2], padded[1:-1, 1:-1, 2:])


def local(phase_field, thermal, velocity, transfer_slope, transfer_offset, transfer_gain):
    density = (1.0 + 9.0 * phase_field.astype(jnp.float32)) * thermal
    stacked = jnp.concatenate([density[None], velocity], axis=0)
    padded_in = padded_2(stacked, (("gz", 1), ("gx", 2), ("gy", 3)), 1)
    density_pad = padded_in[0]
    vel_aboves = [neighbours(padded_in[1 + which], which)[1] for which in range(3)]
    lowers = []
    uppers = []
    rhs = jnp.zeros_like(density)
    for which in range(3):
        front, back = neighbours(density_pad, which)
        front = jnp.where(front > 0.0, front, density)
        back = jnp.where(back > 0.0, back, density)
        lowers.append(2.0 / (density + front))
        uppers.append(2.0 / (density + back))
        rhs = rhs - (vel_aboves[which] - velocity[which])
    inverse = 1.0 / (lowers[0] + uppers[0] + lowers[1] + uppers[1] + lowers[2] + uppers[2])
    pad_shape = (density.shape[0] + 2, density.shape[1] + 2, density.shape[2] + 2)
    pressure_pad = jnp.zeros(pad_shape, jnp.float32)
    residual = rhs

    def precond_sum(resid, cond):
        return lax.psum(jnp.sum(resid * cond), ("gz", "gx", "gy"))

    precond = inverse * residual
    direction = precond
    norm_now = precond_sum(residual, precond)
    for iteration in range(ITERS):
        padded = padded_2(direction, (("gz", 0), ("gx", 1), ("gy", 2)), 1)
        total = jnp.zeros_like(direction)
        for operate_which in range(3):
            operate_front, operate_back = neighbours(padded, operate_which)
            total = total + lowers[operate_which] * (direction - operate_front)
            total = total + uppers[operate_which] * (direction - operate_back)
        alpha = norm_now / lax.psum(jnp.sum(direction * total), ("gz", "gx", "gy"))
        pressure_pad = pressure_pad + alpha * padded
        residual = residual - alpha * total
        if iteration + 1 < ITERS:
            precond = inverse * residual
            norm_next = precond_sum(residual, precond)
            direction = precond + norm_next / norm_now * direction
            norm_now = norm_next
    pressure = inner(pressure_pad)
    pieces = []
    for which in range(3):
        front, unused = neighbours(pressure_pad, which)
        pieces.append(velocity[which] - lowers[which] * (pressure - front))
    corrected = jnp.stack(pieces)
    scalar = pieces[0] + pieces[1] + pieces[2]
    depth_total = jnp.float32(density.shape[0] * lax.axis_size("gz"))

    def render(index):
        slope = transfer_slope[index]
        offset = transfer_offset[index]
        opacity = transfer_gain[index] / depth_total * jax.nn.sigmoid(slope[3] * scalar + offset[3])
        keep = 1.0 - opacity
        inclusive = jnp.cumprod(keep, axis=0)
        passed = jnp.concatenate([jnp.ones_like(inclusive[:1]), inclusive[:-1]], axis=0)
        weight = passed * opacity
        planes = jnp.stack(
            [
                jnp.sum(weight * jax.nn.sigmoid(slope[channel] * scalar + offset[channel]), axis=0)
                for channel in range(3)
            ]
        )
        return (planes, inclusive[-1])

    colors, through = lax.map(render, jnp.arange(transfer_slope.shape[0]))

    def multiply(earlier, later):
        return earlier * later

    before = prefix(through, "gz", multiply, jnp.ones_like(through))
    terms = jnp.concatenate([before[:, None] * colors, (before * (1.0 - through))[:, None]], axis=1)
    images = lax.psum_scatter(terms, "gz", scatter_dimension=0, tiled=True)
    return (corrected, images)


def solution(mesh):
    return jax.shard_map(
        local,
        mesh=mesh,
        in_specs=(
            P("gz", "gx", "gy"),
            P("gz", "gx", "gy"),
            P(None, "gz", "gx", "gy"),
            P(),
            P(),
            P(),
        ),
        out_specs=(P(None, "gz", "gx", "gy"), P("gz", None, "gx", "gy")),
        check_vma=False,
    )
```

profile of v0, /device:TPU:6, one launch (start us, length us, event | category | flops | bytes accessed | tf_op | source)
XLA Modules:
  0.0 1011.5 jit_solution(11295659859310249361)
XLA Ops:
  8.2 3.5 collective-permute-start
  11.7 1.3 collective-permute-start.1
  13.2 4.2 collective-permute-done.1
  17.5 1.9 collective-permute-start.2
  19.4 3.6 collective-permute-start.3
  23.1 1.4 collective-permute-done.3
  24.8 4.3 collective-permute-start.4
  30.4 7.4 collective-permute-done.4
  37.9 4.8 collective-permute-done.5
  43.5 3.5 collective-permute-start.6
  48.4 4.5 collective-permute-done.7
  52.9 1.9 collective-permute-start.8
  54.9 3.8 collective-permute-start.9
  58.7 1.3 collective-permute-done.9
  60.2 4.3 collective-permute-start.10
  66.9 5.9 collective-permute-done.11
  73.5 100.6 %all-reduce.1 = (f32[]{:T(128)}, f32[]{:T(128)}) all-reduce(f32[]{:T(128)} %get-tuple-element.146, f32[]{:T(128)} %get-tuple-element.145), channel_id=1, replica_groups=mesh['gx'=8,'gy'=8,'gz'=8] {'gz','gx','gy'}, use_global_device_ids=true, to_apply=%region_1.2 | all-reduce | flops 2 | bytes 16 | tf_op jit(solution)/shard_map/psum | solution.py:73
  176.1 96.3 %psum.58 = f32[]{:T(128)} all-reduce(f32[]{:T(128)} %get-tuple-element.184), channel_id=1, replica_groups=mesh['gx'=8,'gy'=8,'gz'=8] {'gz','gx','gy'}, use_global_device_ids=true, to_apply=%region_5.6 | all-reduce | flops 1 | bytes 8 | tf_op jit(solution)/shard_map/psum | solution.py:73
  273.8 3.4 collective-permute-start.12
  278.6 4.2 collective-permute-done.13
  282.8 1.9 collective-permute-start.14
  284.7 3.6 collective-permute-start.15
  288.4 1.3 collective-permute-done.15
  289.8 2.5 collective-permute-start.16
  294.7 4.4 collective-permute-done.17
  299.8 99.1 %psum.59 = f32[]{:T(128)} all-reduce(f32[]{:T(128)} %get-tuple-element.182), channel_id=1, replica_groups=mesh['gx'=8,'gy'=8,'gz'=8] {'gz','gx','gy'}, use_global_device_ids=true, to_apply=%region_7.8 | all-reduce | flops 1 | bytes 8 | tf_op jit(solution)/shard_map/psum | solution.py:85
  400.8 95.3 %psum.60 = f32[]{:T(128)} all-reduce(f32[]{:T(128)} %get-tuple-element.179), channel_id=1, replica_groups=mesh['gx'=8,'gy'=8,'gz'=8] {'gz','gx','gy'}, use_global_device_ids=true, to_apply=%region_9.10 | all-reduce | flops 1 | bytes 8 | tf_op jit(solution)/shard_map/psum | solution.py:73
  497.5 2.2 collective-permute-start.18
  501.1 4.4 collective-permute-done.19
  505.5 1.9 collective-permute-start.20
  507.4 3.6 collective-permute-start.21
  511.0 1.3 collective-permute-done.21
  512.5 3.0 collective-permute-start.22
  517.9 4.4 collective-permute-done.23
  523.0 99.0 %psum.61 = f32[]{:T(128)} all-reduce(f32[]{:T(128)} %get-tuple-element.177), channel_id=1, replica_groups=mesh['gx'=8,'gy'=8,'gz'=8] {'gz','gx','gy'}, use_global_device_ids=true, to_apply=%region_11.12 | all-reduce | flops 1 | bytes 8 | tf_op jit(solution)/shard_map/psum | solution.py:85
  624.0 95.3 %psum.62 = f32[]{:T(128)} all-reduce(f32[]{:T(128)} %multiply_reduce_fusion.3), channel_id=1, replica_groups=mesh['gx'=8,'gy'=8,'gz'=8] {'gz','gx','gy'}, use_global_device_ids=true, to_apply=%region_13.14 | all-reduce | flops 1 | bytes 8 | tf_op jit(solution)/shard_map/psum | solution.py:73
  720.7 2.1 collective-permute-start.24
  722.8 1.3 collective-permute-start.25
  724.1 4.5 collective-permute-done.25
  728.7 1.9 collective-permute-start.26
  730.6 3.6 collective-permute-start.27
  734.2 1.3 collective-permute-done.27
  735.7 3.0 collective-permute-start.28
  741.1 4.4 collective-permute-done.29
  746.2 99.0 %psum.63 = f32[]{:T(128)} all-reduce(f32[]{:T(128)} %fusion.30), channel_id=1, replica_groups=mesh['gx'=8,'gy'=8,'gz'=8] {'gz','gx','gy'}, use_global_device_ids=true, to_apply=%region_15.16 | all-reduce | flops 1 | bytes 8 | tf_op jit(solution)/shard_map/psum | solution.py:85
  848.0 91.7 %while.28 = (s32[]{:T(128)}, f32[8,3,16,128]{3,2,1,0:T(8,128)S(1)}, f32[8,16,128]{2,1,0:T(8,128)S(1)}, s32[8]{0:T(128)S(1)}, f32[8]{0:T(128)S(1)}, /*index=5*/f3...) while((s32[]{:T(128)}, f32[8,3,16,128]{3,2,1,0:T(8,128)S(1)}, ...), condition=%wide.region_21.22_spmd.clone, body=%wide.region_16.21_spmd.sunk.clone | while | flops 694278 | bytes 459103 | solution.py:118
  853.0 1.3 fusion.138
  854.4 5.1 multiply_reduce_fusion.12
  864.5 1.3 fusion.138
  865.8 5.1 multiply_reduce_fusion.12
  876.0 1.3 fusion.138
  877.3 5.1 multiply_reduce_fusion.12
  887.4 1.3 fusion.138
  888.7 5.1 multiply_reduce_fusion.12
  898.9 1.3 fusion.138
  900.2 5.1 multiply_reduce_fusion.12
  910.4 1.3 fusion.138
  911.7 5.1 multiply_reduce_fusion.12
  921.8 1.3 fusion.138
  923.1 5.1 multiply_reduce_fusion.12
  933.3 1.3 fusion.138
  934.6 5.1 multiply_reduce_fusion.12
  939.7 25.5 %all-gather = f32[64,16,128]{2,1,0:T(8,128)S(1)} all-gather(f32[8,16,128]{2,1,0:T(8,128)S(1)} %get-tuple-element.124), channel_id=2, replica_groups=mesh['gx'=8,'gy'=8,'gz'=8] {'gz'}, dimensions={0}, use_global_device_ids=true | all-gather | bytes 589824 | tf_op jit(solution)/shard_map/all_gather | solution.py:28
  967.0 37.6 %reduce-scatter.2.cloned.1.call-done = f32[1,4,16,128]{3,2,1,0:T(8,128)} async-done(((f32[8,4,16,128]{3,2,1,0:T(8,128)}), f32[1,4,16,128]{3,2,1,0:T(8,128)}) %reduce-scatter.2.cloned.1.call-update) | async-done | bytes 32784 | tf_op jit(solution)/shard_map/reduce_scatter | solution.py:125
  (149 shorter events, 45.7 us)
Async XLA Ops:
  7.2 1.0 copy-start
  7.2 997.5 %reduce-scatter.2.cloned.1.call-start = ((), (), s32[]{:S(2)}) async-start(), calls=%async_computation.1 | async-start | bytes 294912 | tf_op jit(solution)/shard_map/reduce_scatter | solution.py:125
  8.2 5.1 collective-permute-start
  11.7 5.8 collective-permute-start.1
  17.5 5.6 collective-permute-start.2
  19.4 5.1 collective-permute-start.3
  24.8 13.0 %collective-permute-start.4 = (f32[4,10,18,1]{3,2,1,0:T(8,128)S(1)}, f32[4,10,18,1]{3,2,1,0:T(8,128)S(1)}, u32[]{:S(2)}, u32[]{:S(2)}) collective-permute-start(f32[4,10,18,1]{3,2,1,0:T(8,128)S(1)} %get-tuple-element.211), channel_id=1, source_target_pairs={{0,8},{8,16},{16,24},{24,32},{32,40},{40,48},{48,56},{1,9},{9,17},... | collective-permute-start | bytes 8648 | tf_op jit(solution)/shard_map/ppermute | solution.py:17
  29.1 13.5 %collective-permute-start.5 = (f32[4,10,18,1]{3,2,1,0:T(8,128)S(1)}, f32[4,10,18,1]{3,2,1,0:T(8,128)S(1)}, u32[]{:S(2)}, u32[]{:S(2)}) collective-permute-start(f32[4,10,18,1]{3,2,1,0:T(8,128)S(1)} %get-tuple-element.212), channel_id=1, source_target_pairs={{8,0},{16,8},{24,16},{32,24},{40,32},{48,40},{56,48},{9,1},{17,9},... | collective-permute-start | bytes 8648 | tf_op jit(solution)/shard_map/ppermute | solution.py:19
  43.5 4.8 collective-permute-start.6
  47.0 5.9 collective-permute-start.7
  52.9 5.8 collective-permute-start.8
  54.9 5.2 collective-permute-start.9
  60.2 6.7 collective-permute-start.10
  64.4 8.3 collective-permute-start.11
  273.8 4.8 collective-permute-start.12
  277.2 5.5 collective-permute-start.13
  282.8 5.6 collective-permute-start.14
  284.7 5.0 collective-permute-start.15
  289.8 4.9 collective-permute-start.16
  292.3 6.8 collective-permute-start.17
  497.5 3.6 collective-permute-start.18
  499.7 5.7 collective-permute-start.19
  505.5 5.6 collective-permute-start.20
  507.4 5.0 collective-permute-start.21
  512.5 5.4 collective-permute-start.22
  515.5 6.8 collective-permute-start.23
  720.7 3.5 collective-permute-start.24
  722.8 5.9 collective-permute-start.25
  728.7 5.6 collective-permute-start.26
  730.6 5.0 collective-permute-start.27
  735.7 5.4 collective-permute-start.28
  738.7 6.8 collective-permute-start.29
  847.2 0.7 copy-start.2
  847.3 0.7 copy-start.1
  847.4 0.7 copy-start.3
Sparse Core Ops, SparseCore 0:
  966.4 38.1 reduce-scatter.1
where the time goes:
time: 1010 us
  blocking collectives  710 us (70%)
  waiting for transfers between devices  102 us (10%)
  starting transfers between devices  72.8 us (7%)
  other arithmetic  60.3 us (6%)
  between operations  24 us (2%)
  loops' own time  21.3 us (2%)
  local copies, waits for them, and re-layouts  20.8 us (2%)
    psum x4, blocking collectives, precond_sum(): return lax.psum(jnp.sum(resid * cond), ('gz', 'gx', 'gy'))  388 us
    psum x3, blocking collectives, local(): alpha = norm_now / lax.psum(jnp.sum(direction * total), ('gz', 'gx', 'gy'))  297 us
    ppermute x15, waiting for transfers between devices, padded_2(): lax.ppermute(head, axis, [((i + 1) % count, i) for i in range(ends)])  52.2 us
    ppermute x15, starting transfers between devices, padded_2(): lax.ppermute(tail, axis, [(i, (i + 1) % count) for i in range(ends)])  41.4 us
    reduce_sum x8, other arithmetic, render(): jnp.sum(weight * jax.nn.sigmoid(slope[channel] * scalar + offset[channel]...  40.6 us
    reduce_scatter x1, waiting for transfers between devices, local(): images = lax.psum_scatter(terms, 'gz', scatter_dimension=0, tiled=True)  37.6 us
    ppermute x15, starting transfers between devices, padded_2(): lax.ppermute(head, axis, [((i + 1) % count, i) for i in range(ends)])  31.3 us
    all_gather x1, blocking collectives, prefix(): everything = lax.all_gather(value, axis)  25.5 us
  transfers between devices with their start and end apart: 31, of which 22 were waited for; matrix products, arithmetic and copies ran while one was open for 0% of the time, Pallas kernels for 0%

commit v1 on v0

v1 whole, which is shorter than its diff:
```python
import functools

import jax
import jax.numpy as jnp
from jax import lax
from jax.experimental import pallas as pl
from jax.experimental.pallas import tpu as pltpu
from jax.sharding import PartitionSpec as P

MESH = pl.DeviceIdType.MESH
Z, X, Y = 8, 16, 128
R = Z * X
K = R // 8
TF = 8
PAD = 8
FAR_FIRST = (4, 3, 5, 2, 6, 1, 7)


def lanes(shape):
    return lax.broadcasted_iota(jnp.int32, shape, 1)


def group(v, k):
    return v[8 * k : 8 * k + 8]


def recip(v):
    r = pl.reciprocal(v, approx=True)
    r = r * (2.0 - v * r)
    return r * (2.0 - v * r)


def pack_ends(v):
    lane = lanes((8, Y))
    out = jnp.zeros((8, Y), jnp.float32)
    for k in range(K):
        out = jnp.where(lane // 2 == k, pltpu.roll(group(v, k), 2 * k + 1, 1), out)
    return out


def unpack_ends(below, above):
    lane = lanes((8, Y))
    both = jnp.where(lane % 2 == 0, pltpu.roll(above, Y - 1, 1), pltpu.roll(below, 1, 1))
    return jnp.concatenate([pltpu.roll(both, Y - (2 * k + 1), 1) for k in range(K)], axis=0)


def spread(below, above):
    pieces = []
    for z in range(Z):
        pieces.append(jnp.broadcast_to(below[z : z + 1], (8, Y)))
        pieces.append(jnp.broadcast_to(above[z : z + 1], (8, Y)))
    return jnp.concatenate(pieces, axis=0)


def kernel(
    sizes,
    phase_in,
    thermal_in,
    vel_in,
    slope,
    offset,
    gain,
    corrected,
    images,
    phase_v,
    thermal_v,
    vel_v,
    vel1_pad,
    den_pad,
    s1z,
    s1x,
    s1xu,
    s1y,
    h1,
    v_pad,
    coef,
    edge_z,
    sx,
    sy,
    h,
    grads,
    row_send,
    row_recv,
    scal_v,
    scal_send,
    scal_recv,
    img_send,
    img_recv,
    in_sem,
    send_sem,
    recv_sem,
):
    nx, ny, nz = sizes
    ix, iy, iz = lax.axis_index("gx"), lax.axis_index("gy"), lax.axis_index("gz")
    xm, xp = {"gx": lax.rem(ix + nx - 1, nx)}, {"gx": lax.rem(ix + 1, nx)}
    ym, yp = {"gy": lax.rem(iy + ny - 1, ny)}, {"gy": lax.rem(iy + 1, ny)}
    zm, zp = {"gz": lax.rem(iz + nz - 1, nz)}, {"gz": lax.rem(iz + 1, nz)}
    x_first, x_last = ix == 0, ix == nx - 1
    y_first, y_last = iy == 0, iy == ny - 1
    z_first, z_last = iz == 0, iz == nz - 1

    loads = [
        pltpu.make_async_copy(phase_in, phase_v, in_sem.at[0]),
        pltpu.make_async_copy(thermal_in, thermal_v, in_sem.at[1]),
        pltpu.make_async_copy(vel_in, vel_v, in_sem.at[2]),
    ]
    for copy in loads:
        copy.start()

    barrier = pltpu.get_barrier_semaphore()
    greeted = 0
    for name, here, count in (("gx", ix, nx), ("gy", iy, ny), ("gz", iz, nz)):
        for k in range(1, count):
            pl.semaphore_signal(
                barrier, inc=1, device_id={name: lax.rem(here + k, count)}, device_id_type=MESH
            )
            greeted += 1

    pad = jnp.zeros((PAD, Y), jnp.float32)
    for ref in [den_pad, vel1_pad] + [v_pad.at[j] for j in range(4)]:
        ref[0:PAD] = pad
        ref[PAD + R : PAD + R + PAD] = pad

    def send(src, dst, group_id, device):
        pltpu.make_async_remote_copy(
            src, dst, send_sem.at[group_id], recv_sem.at[group_id], device_id=device, device_id_type=MESH
        ).start()

    def whole(ref, group_id):
        return pltpu.make_async_remote_copy(
            ref, ref, send_sem.at[group_id], recv_sem.at[group_id], device_id=xp, device_id_type=MESH
        )

    lane = lanes((R, Y))
    row = lax.broadcasted_iota(jnp.int32, (R, Y), 0)
    in_x = row % X

    for copy in loads:
        copy.wait()
    den = (1.0 + 9.0 * phase_v[...].astype(jnp.float32)) * thermal_v[...]
    den_pad[PAD : PAD + R] = den
    vel0, vel1, vel2 = vel_v[0:R], vel_v[R : 2 * R], vel_v[2 * R : 3 * R]
    vel1_pad[PAD : PAD + R] = vel1
    s1z[0:X] = den[0:X]
    s1z[X : 2 * X] = vel0[0:X]
    s1x[0:8] = den_pad[pl.ds(PAD, 8, stride=X)]
    s1x[8:16] = vel1_pad[pl.ds(PAD, 8, stride=X)]
    s1xu[...] = den_pad[pl.ds(PAD + X - 1, 8, stride=X)]
    ends = pack_ends(den)
    lane8 = lanes((8, Y))
    for k in range(K):
        ends = jnp.where(lane8 == 2 * K + k, pltpu.roll(group(vel2, k), 2 * K + k, 1), ends)
    s1y[...] = ends

    pl.semaphore_wait(barrier, greeted)

    send(den_pad.at[pl.ds(PAD + R - X, X)], h1.at[pl.ds(0, 16)], 0, zp)
    send(s1z, h1.at[pl.ds(16, 32)], 0, zm)
    send(s1xu, h1.at[pl.ds(48, 8)], 0, xp)
    send(s1x, h1.at[pl.ds(56, 16)], 0, xm)
    send(s1y, h1.at[pl.ds(72, 8)], 0, yp)
    send(s1y, h1.at[pl.ds(80, 8)], 0, ym)
    whole(h1, 0).wait_recv()

    def face(first, own, other):
        return jnp.where(first, own, other)

    zb = jnp.concatenate([face(z_first, den[0:X], h1[0:16]), den[: R - X]], axis=0)
    za = jnp.concatenate([den[X:], face(z_last, den[R - X :], h1[16:32])], axis=0)
    bx = spread(h1[48:56], h1[56:64])
    xb = jnp.where(in_x == 0, face(x_first, den, bx), den_pad[PAD - 1 : PAD - 1 + R])
    xa = jnp.where(in_x == X - 1, face(x_last, den, bx), den_pad[PAD + 1 : PAD + 1 + R])
    by = unpack_ends(h1[72:80], h1[80:88])
    yb = jnp.where(lane == 0, face(y_first, den, by), pltpu.roll(den, 1, 1))
    ya = jnp.where(lane == Y - 1, face(y_last, den, by), pltpu.roll(den, Y - 1, 1))
    low_z, up_z = 2.0 * recip(den + zb), 2.0 * recip(den + za)
    low_x, up_x = 2.0 * recip(den + xb), 2.0 * recip(den + xa)
    low_y, up_y = 2.0 * recip(den + yb), 2.0 * recip(den + ya)
    inverse = recip(low_z + up_z + low_x + up_x + low_y + up_y)

    def keep(flag):
        return jnp.where(flag, 0.0, 1.0)

    zero = jnp.zeros((R, Y), jnp.float32)
    coef[0] = low_z
    coef[1] = low_x
    coef[2] = low_y
    coef[3] = up_z
    coef[4] = jnp.where(in_x == X - 1, 0.0, up_x)
    coef[5] = jnp.where(lane == Y - 1, 0.0, up_y)
    coef[6] = jnp.where(in_x == 0, 0.0, low_x)
    coef[7] = jnp.where(lane == 0, 0.0, low_y)
    coef[8] = jnp.where(
        in_x == 0, low_x * keep(x_first), jnp.where(in_x == X - 1, up_x * keep(x_last), zero)
    )
    coef[9] = jnp.where(
        lane == 0, low_y * keep(y_first), jnp.where(lane == Y - 1, up_y * keep(y_last), zero)
    )
    coef[10] = inverse
    edge_z[0:X] = low_z[0:X] * keep(z_first)
    edge_z[X : 2 * X] = up_z[R - X :] * keep(z_last)

    above0 = jnp.concatenate([vel0[X:], h1[32:48] * keep(z_last)], axis=0)
    bv = spread(h1[56:64], h1[64:72])
    above1 = jnp.where(in_x == X - 1, bv * keep(x_last), vel1_pad[PAD + 1 : PAD + 1 + R])
    ends_above = h1[80:88]
    bw = jnp.concatenate(
        [pltpu.roll(ends_above, Y - 1 - (2 * K + k), 1) for k in range(K)], axis=0
    )
    above2 = jnp.where(lane == Y - 1, bw * keep(y_last), pltpu.roll(vel2, Y - 1, 1))
    rhs = -(((above0 - vel0) + (above1 - vel1)) + (above2 - vel2))

    def total(v):
        return jnp.sum(v.reshape(K, 8, Y), axis=0)

    sums = []
    scaled = rhs
    for j in range(4):
        v = coef[10] * scaled
        own = v_pad.at[j]
        own[PAD : PAD + R] = v
        sx[j, 0:8] = own[pl.ds(PAD, 8, stride=X)]
        sx[j, 8:16] = own[pl.ds(PAD + X - 1, 8, stride=X)]
        sy[j] = pack_ends(v)
        hj = h.at[j]
        send(own.at[pl.ds(PAD + R - X, X)], hj.at[pl.ds(0, 16)], 1 + j, zp)
        send(own.at[pl.ds(PAD, X)], hj.at[pl.ds(16, 16)], 1 + j, zm)
        send(sx.at[j, pl.ds(8, 8)], hj.at[pl.ds(32, 8)], 1 + j, xp)
        send(sx.at[j, pl.ds(0, 8)], hj.at[pl.ds(40, 8)], 1 + j, xm)
        send(sy.at[j], hj.at[pl.ds(48, 8)], 1 + j, yp)
        send(sy.at[j], hj.at[pl.ds(56, 8)], 1 + j, ym)

        sums.append(total(scaled * v))
        z_low = coef[0, X:R] * v[: R - X]
        z_up = coef[3, 0 : R - X] * v[X:]
        x_low = coef[6] * own[PAD - 1 : PAD - 1 + R]
        x_up = coef[4] * own[PAD + 1 : PAD + 1 + R]
        y_low = coef[7] * pltpu.roll(v, 1, 1)
        y_up = coef[5] * pltpu.roll(v, Y - 1, 1)
        rest = (x_low + x_up) + (y_low + y_up)

        whole(hj, 1 + j).wait_recv()
        z_low = jnp.concatenate([edge_z[0:X] * hj[0:16], z_low], axis=0)
        z_up = jnp.concatenate([z_up, edge_z[X : 2 * X] * hj[16:32]], axis=0)
        x_edge = coef[8] * spread(hj[32:40], hj[40:48])
        y_edge = coef[9] * unpack_ends(hj[48:56], hj[56:64])
        image = ((z_low + z_up) + rest) + (x_edge + y_edge)
        sums.append(total(v * image))

        g0 = coef[0] * v - z_low
        g1 = coef[1] * v - x_low - jnp.where(in_x == 0, x_edge, 0.0)
        g2 = coef[2] * v - y_low - jnp.where(lane == 0, y_edge, 0.0)
        grads[j, 0] = g0
        grads[j, 1] = g1
        grads[j, 2] = g2
        grads[j, 3] = g0 + g1 + g2
        scaled = image

    folded = jnp.zeros((8, Y), jnp.float32)
    for m, value in enumerate(sums):
        value = value + pltpu.roll(value, 64, 1)
        value = value + pltpu.roll(value, 32, 1)
        value = value + pltpu.roll(value, 16, 1)
        folded = jnp.where(lane8 // 16 == m, value, folded)
    line = jnp.sum(folded, axis=0, keepdims=True)
    for stage, (name, here, count) in enumerate((("gx", ix, nx), ("gy", iy, ny), ("gz", iz, nz))):
        row_send[stage] = line
        for k in FAR_FIRST:
            if k < count:
                send(
                    row_send.at[stage],
                    row_recv.at[stage, k - 1],
                    5 + stage,
                    {name: lax.rem(here + k, count)},
                )
        whole(row_recv.at[stage, pl.ds(0, count - 1)], 5 + stage).wait_recv()
        for k in range(count - 1):
            line = line + row_recv[stage, k]
    lane1 = lanes((1, Y))
    m = [jnp.sum(jnp.where(lane1 // 16 == i, line, 0.0), axis=1, keepdims=True) for i in range(8)]

    a = [[m[i + j] - m[i + j + 1] for j in range(4)] for i in range(4)]
    b = [m[i] for i in range(4)]
    pivots = []
    for p in range(4):
        ok = a[p][p] > 1e-7 * (m[2 * p] - m[2 * p + 1])
        pivots.append(jnp.where(ok, 1.0 / jnp.where(ok, a[p][p], 1.0), 0.0))
        for i in range(p + 1, 4):
            factor = a[p][i] * pivots[p]
            for j in range(i, 4):
                a[i][j] = a[i][j] - factor * a[p][j]
            b[i] = b[i] - factor * b[p]
    c = [None] * 4
    for p in reversed(range(4)):
        value = b[p]
        for j in range(p + 1, 4):
            value = value - a[p][j] * c[j]
        c[p] = value * pivots[p]

    vel = [vel_v[d * R : (d + 1) * R] for d in range(3)]
    scalar = vel[0] + vel[1] + vel[2]
    for j in range(4):
        scalar = scalar - c[j] * grads[j, 3]
    scal_v[...] = scalar
    for t in range(TF):
        scal_send[t, 0:8] = scal_v[pl.ds(t, 8, stride=8)]
        scal_send[t, 8:16] = scal_v[pl.ds(R // 2 + t, 8, stride=8)]
    for k in FAR_FIRST:
        to = lax.rem(iz + k, nz)
        send(scal_send.at[to], scal_recv.at[pl.ds(iz * 16, 16)], 8, {"gz": to})
    scal_recv[pl.ds(pl.multiple_of(iz * 16, 16), 16)] = scal_send[iz]
    for d in range(3):
        value = vel[d]
        for j in range(4):
            value = value - c[j] * grads[j, d]
        corrected[d * R : (d + 1) * R] = value
    whole(scal_recv.at[pl.ds(0, 16 * (nz - 1))], 8).wait_recv()

    field = [
        jnp.concatenate([scal_recv[pl.ds(2 * z + r, 8, stride=16)] for r in range(2)], axis=0)
        for z in range(Z)
    ]
    sub = lax.broadcasted_iota(jnp.int32, (8, Y), 0)
    for k in FAR_FIRST + (0,):
        t = lax.rem(iz + k, nz)
        half = 0.5 / (Z * nz) * gain[t]
        slopes = [0.5 * slope[t, i] for i in range(4)]
        offsets = [0.5 * offset[t, i] for i in range(4)]
        through = jnp.ones((16, Y), jnp.float32)
        colors = [jnp.zeros((16, Y), jnp.float32) for _ in range(3)]
        for z in range(Z):
            weight = through * (half + half * jnp.tanh(slopes[3] * field[z] + offsets[3]))
            through = through - weight
            for i in range(3):
                colors[i] = colors[i] + weight * jnp.tanh(slopes[i] * field[z] + offsets[i])
        lines = [[None, None] for _ in range(4)]
        for r in range(2):
            here = through[8 * r : 8 * r + 8]
            before = jnp.where(sub >= 1, pltpu.roll(here, 1, 0), 1.0)
            for step in (1, 2, 4):
                before = before * jnp.where(sub >= step, pltpu.roll(before, step, 0), 1.0)
            for i in range(3):
                color = 0.5 * (colors[i][8 * r : 8 * r + 8] + (1.0 - here))
                lines[i][r] = jnp.sum(before * color, axis=0, keepdims=True)
            lines[3][r] = (1.0 - before * here)[7:8]
        tile = jnp.concatenate([lines[i][r] for i in range(4) for r in range(2)], axis=0)
        if k:
            img_send[t] = tile
            send(img_send.at[t], img_recv.at[pl.ds(iz * 8, 8)], 9, {"gz": t})
        else:
            img_recv[pl.ds(pl.multiple_of(iz * 8, 8), 8)] = tile
    whole(img_recv.at[pl.ds(0, 8 * (nz - 1))], 9).wait_recv()
    for i in range(4):
        for r in range(2):
            images[i * X + 8 * r : i * X + 8 * r + 8] = img_recv[pl.ds(2 * i + r, 8, stride=8)]

    whole(h1, 0).wait_send()
    for j in range(4):
        whole(h.at[j], 1 + j).wait_send()
    for stage, count in enumerate((nx, ny, nz)):
        whole(row_recv.at[stage, pl.ds(0, count - 1)], 5 + stage).wait_send()
    whole(scal_recv.at[pl.ds(0, 16 * (nz - 1))], 8).wait_send()
    whole(img_recv.at[pl.ds(0, 8 * (nz - 1))], 9).wait_send()


def local(sizes, phase_field, thermal, velocity, transfer_slope, transfer_offset, transfer_gain):
    f32 = jnp.float32
    hbm = pl.BlockSpec(memory_space=pl.ANY)
    smem = pl.BlockSpec(memory_space=pltpu.SMEM)
    vmem = pl.BlockSpec(memory_space=pltpu.VMEM)
    corrected, images = pl.pallas_call(
        functools.partial(kernel, sizes),
        out_shape=(
            jax.ShapeDtypeStruct((3 * R, Y), f32),
            jax.ShapeDtypeStruct((4 * X, Y), f32),
        ),
        in_specs=[hbm, hbm, hbm, smem, smem, smem],
        out_specs=(vmem, vmem),
        scratch_shapes=[
            pltpu.VMEM((R, Y), jnp.int32),
            pltpu.VMEM((R, Y), f32),
            pltpu.VMEM((3 * R, Y), f32),
            pltpu.VMEM((R + 2 * PAD, Y), f32),
            pltpu.VMEM((R + 2 * PAD, Y), f32),
            pltpu.VMEM((2 * X, Y), f32),
            pltpu.VMEM((16, Y), f32),
            pltpu.VMEM((8, Y), f32),
            pltpu.VMEM((8, Y), f32),
            pltpu.VMEM((88, Y), f32),
            pltpu.VMEM((4, R + 2 * PAD, Y), f32),
            pltpu.VMEM((11, R, Y), f32),
            pltpu.VMEM((2 * X, Y), f32),
            pltpu.VMEM((4, 16, Y), f32),
            pltpu.VMEM((4, 8, Y), f32),
            pltpu.VMEM((4, 64, Y), f32),
            pltpu.VMEM((4, 4, R, Y), f32),
            pltpu.VMEM((3, 1, Y), f32),
            pltpu.VMEM((3, 7, 1, Y), f32),
            pltpu.VMEM((R, Y), f32),
            pltpu.VMEM((TF, 16, Y), f32),
            pltpu.VMEM((TF * 16, Y), f32),
            pltpu.VMEM((TF, 8, Y), f32),
            pltpu.VMEM((TF * 8, Y), f32),
            pltpu.SemaphoreType.DMA((3,)),
            pltpu.SemaphoreType.DMA((10,)),
            pltpu.SemaphoreType.DMA((10,)),
        ],
        compiler_params=pltpu.CompilerParams(
            collective_id=0, has_side_effects=True, vmem_limit_bytes=16 * 2**20
        ),
    )(
        phase_field.reshape(R, Y),
        thermal.reshape(R, Y),
        velocity.reshape(3 * R, Y),
        transfer_slope,
        transfer_offset,
        transfer_gain,
    )
    return corrected.reshape(3, Z, X, Y), images.reshape(1, 4, X, Y)


def solution(mesh):
    sizes = (mesh.shape["gx"], mesh.shape["gy"], mesh.shape["gz"])
    return jax.shard_map(
        functools.partial(local, sizes),
        mesh=mesh,
        in_specs=(
            P("gz", "gx", "gy"),
            P("gz", "gx", "gy"),
            P(None, "gz", "gx", "gy"),
            P(),
            P(),
            P(),
        ),
        out_specs=(P(None, "gz", "gx", "gy"), P("gz", None, "gx", "gy")),
        check_vma=False,
    )
```

time: 1010 us -> 62.2 us (0.06)
  the two profiles are of different devices: /device:TPU:6 before, /device:TPU:8 now
where the time goes in v1:
time: 62.2 us; the launch traced here: 61.9 us
  Pallas kernels  55.4 us (89%)
  local copies, waits for them, and re-layouts  5.91 us (10%)
  between operations  0.65 us (1%)
    pallas_call x1, Pallas kernels, local(): pl.pallas_call(functools.partial(kernel, sizes), out_shape=(jax.ShapeDtyp...  55.4 us
    unnamed x16, local copies, waits for them, and re-layouts  5.91 us

profile of v1, /device:TPU:8, one launch (start us, length us, event | category | flops | bytes accessed | tf_op | source)
XLA Modules:
  0.0 61.9 jit_solution(15108129969823937786)
XLA Ops:
  0.6 0.0 copy-start.4
  0.6 0.7 %copy-done.4 = f32[8,4]{0,1:T(4,128)S(1)} copy-done((f32[8,4]{0,1:T(4,128)S(1)}, f32[8,4]{0,1:T(4,128)}, u32[]{:S(2)}) %copy-start.4) | copy-done | bytes 152
  1.3 0.0 copy-start.5
  1.3 0.1 copy.8.slope
  1.4 0.6 copy-done.5
  2.0 0.0 copy-start.3
  2.0 0.1 copy.9.offset
  2.1 0.6 copy-done.3
  2.7 0.0 copy-start
  2.7 0.9 %copy-done = f32[3,8,16,128]{3,2,1,0:T(8,128)S(1)} copy-done((f32[3,8,16,128]{3,2,1,0:T(8,128)S(1)}, f32[3,8,16,128]{3,2,1,0:T(8,128)}, u32[]{:S(2)}) %copy-start) | copy-done | bytes 196632
  3.6 0.0 copy-start.1
  3.6 0.8 %copy-done.1 = s32[8,16,128]{2,1,0:T(8,128)S(1)} copy-done((s32[8,16,128]{2,1,0:T(8,128)S(1)}, s32[8,16,128]{2,1,0:T(8,128)}, u32[]{:S(2)}) %copy-start.1) | copy-done | bytes 65560
  4.4 0.0 copy-start.2
  4.4 0.8 %copy-done.2 = f32[8,16,128]{2,1,0:T(8,128)S(1)} copy-done((f32[8,16,128]{2,1,0:T(8,128)S(1)}, f32[8,16,128]{2,1,0:T(8,128)}, u32[]{:S(2)}) %copy-start.2) | copy-done | bytes 65560
  5.3 55.4 %shard_map.77 = (f32[384,128]{1,0:T(8,128)S(1)}, f32[64,128]{1,0:T(8,128)S(1)}) custom-call(s32[128,128]{1,0:T(8,128)S(1)} %bitcast.7, f32[128,128]{1,0:T(8,128)S(1)} %bitcast.8, f32[384,128]{1,0:T(8,128)S(1)} %bitcast.6, f32[8,4]{1,0:T(8,128)S(1)} %copy.8.slope, f32[8,4]{1,0:T(8,128)S(1)} %copy.9.offset, f32[8]{0:T(128)S(1)} %copy-done.3), custom_call_target="tpu_custom_call" | custom-call | tf_op jit(solution)/shard_map/pallas_call | solution.py:371
  60.6 0.7 %copy.12 = f32[3,8,16,128]{3,2,1,0:T(8,128)} copy(f32[3,8,16,128]{3,2,1,0:T(8,128)S(1)} %bitcast.5) | data formatting | bytes 393216
  61.3 0.6 copy.13
Async XLA Ops:
  0.6 0.7 %copy-start.4 = (f32[8,4]{0,1:T(4,128)S(1)}, f32[8,4]{0,1:T(4,128)}, u32[]{:S(2)}) copy-start(f32[8,4]{0,1:T(4,128)} %param.9) | copy-start | bytes 388
  1.3 0.7 %copy-start.5 = (f32[8,4]{0,1:T(4,128)S(1)}, f32[8,4]{0,1:T(4,128)}, u32[]{:S(2)}) copy-start(f32[8,4]{0,1:T(4,128)} %param.10) | copy-start | bytes 388
  2.0 0.7 %copy-start.3 = (f32[8]{0:T(128)S(1)}, f32[8]{0:T(128)}, u32[]{:S(2)}) copy-start(f32[8]{0:T(128)} %gain.1) | copy-start | bytes 100
  2.7 0.9 %copy-start = (f32[3,8,16,128]{3,2,1,0:T(8,128)S(1)}, f32[3,8,16,128]{3,2,1,0:T(8,128)}, u32[]{:S(2)}) copy-start(f32[3,8,16,128]{3,2,1,0:T(8,128)} %param.8) | copy-start | bytes 589828
  3.6 0.8 %copy-start.1 = (s32[8,16,128]{2,1,0:T(8,128)S(1)}, s32[8,16,128]{2,1,0:T(8,128)}, u32[]{:S(2)}) copy-start(s32[8,16,128]{2,1,0:T(8,128)} %param.6) | copy-start | bytes 196612
  4.4 0.8 %copy-start.2 = (f32[8,16,128]{2,1,0:T(8,128)S(1)}, f32[8,16,128]{2,1,0:T(8,128)}, u32[]{:S(2)}) copy-start(f32[8,16,128]{2,1,0:T(8,128)} %param.7) | copy-start | bytes 196612

commit v2 on v1

--- a/solution.py
+++ b/solution.py
@@ -57,11 +57,14 @@
     phase_in,
     thermal_in,
     vel_in,
+    slope_in,
+    offset_in,
+    gain_in,
+    corrected,
+    images,
     slope,
     offset,
     gain,
-    corrected,
-    images,
     phase_v,
     thermal_v,
     vel_v,
@@ -81,9 +84,13 @@
     grads,
     row_send,
     row_recv,
-    scal_v,
-    scal_send,
-    scal_recv,
+    send_a,
+    send_b,
+    send_c,
+    recv_a,
+    recv_b,
+    recv_c,
+    vel_sum,
     img_send,
     img_recv,
     in_sem,
@@ -104,17 +111,16 @@
         pltpu.make_async_copy(thermal_in, thermal_v, in_sem.at[1]),
         pltpu.make_async_copy(vel_in, vel_v, in_sem.at[2]),
     ]
-    for copy in loads:
+    params = [
+        pltpu.make_async_copy(slope_in, slope, in_sem.at[3]),
+        pltpu.make_async_copy(offset_in, offset, in_sem.at[4]),
+        pltpu.make_async_copy(gain_in, gain, in_sem.at[5]),
+    ]
+    barrier = pltpu.get_barrier_semaphore()
+    for device in (zm, zp, ym, yp, xm, xp):
+        pl.semaphore_signal(barrier, inc=1, device_id=device, device_id_type=MESH)
+    for copy in loads + params:
         copy.start()
-
-    barrier = pltpu.get_barrier_semaphore()
-    greeted = 0
-    for name, here, count in (("gx", ix, nx), ("gy", iy, ny), ("gz", iz, nz)):
-        for k in range(1, count):
-            pl.semaphore_signal(
-                barrier, inc=1, device_id={name: lax.rem(here + k, count)}, device_id_type=MESH
-            )
-            greeted += 1
 
     pad = jnp.zeros((PAD, Y), jnp.float32)
     for ref in [den_pad, vel1_pad] + [v_pad.at[j] for j in range(4)]:
@@ -152,7 +158,7 @@
         ends = jnp.where(lane8 == 2 * K + k, pltpu.roll(group(vel2, k), 2 * K + k, 1), ends)
     s1y[...] = ends
 
-    pl.semaphore_wait(barrier, greeted)
+    pl.semaphore_wait(barrier, 6)
 
     send(den_pad.at[pl.ds(PAD + R - X, X)], h1.at[pl.ds(0, 16)], 0, zp)
     send(s1z, h1.at[pl.ds(16, 32)], 0, zm)
@@ -210,59 +216,99 @@
     above2 = jnp.where(lane == Y - 1, bw * keep(y_last), pltpu.roll(vel2, Y - 1, 1))
     rhs = -(((above0 - vel0) + (above1 - vel1)) + (above2 - vel2))
 
-    def total(v):
-        return jnp.sum(v.reshape(K, 8, Y), axis=0)
-
-    sums = []
+    def hand_out(buf, recv, group_id, steps):
+        rows = buf.shape[1]
+        for k in steps:
+            to = lax.rem(iz + k, nz)
+            send(buf.at[to], recv.at[pl.ds(iz * rows, rows)], group_id, {"gz": to})
+
+    def scatter(fields, buf, recv, group_id, steps):
+        for q, ref in enumerate(fields):
+            for t in range(TF):
+                for r in range(2):
+                    at = 16 * q + 8 * r
+                    buf[t, at : at + 8] = ref[pl.ds(r * (R // 2) + t, 8, stride=8)]
+        rows = 16 * len(fields)
+        hand_out(buf, recv, group_id, steps)
+        recv[pl.ds(pl.multiple_of(iz * rows, rows), rows)] = buf[iz]
+
+    folded = []
+
+    def fold(value):
+        value = jnp.sum(value.reshape(K, 8, Y), axis=0)
+        for step in (64, 32, 16):
+            value = value + pltpu.roll(value, step, 1)
+        m = len(folded)
+        before = folded[-1] if folded else jnp.zeros((8, Y), jnp.float32)
+        folded.append(jnp.where(lane8 // 16 == m, value, before))
+
+    def gradient(j, v, z_low, x_low, y_low):
+        g0, g1, g2 = coef[0] * v - z_low, coef[1] * v - x_low, coef[2] * v - y_low
+        grads[j, 0] = g0
+        grads[j, 1] = g1
+        grads[j, 2] = g2
+        grads[j, 3] = g0 + g1 + g2
+
+    vel_sum[...] = vel0 + vel1 + vel2
     scaled = rhs
+    last = None
     for j in range(4):
         v = coef[10] * scaled
         own = v_pad.at[j]
         own[PAD : PAD + R] = v
-        sx[j, 0:8] = own[pl.ds(PAD, 8, stride=X)]
         sx[j, 8:16] = own[pl.ds(PAD + X - 1, 8, stride=X)]
         sy[j] = pack_ends(v)
         hj = h.at[j]
         send(own.at[pl.ds(PAD + R - X, X)], hj.at[pl.ds(0, 16)], 1 + j, zp)
-        send(own.at[pl.ds(PAD, X)], hj.at[pl.ds(16, 16)], 1 + j, zm)
-        send(sx.at[j, pl.ds(8, 8)], hj.at[pl.ds(32, 8)], 1 + j, xp)
-        send(sx.at[j, pl.ds(0, 8)], hj.at[pl.ds(40, 8)], 1 + j, xm)
-        send(sy.at[j], hj.at[pl.ds(48, 8)], 1 + j, yp)
-        send(sy.at[j], hj.at[pl.ds(56, 8)], 1 + j, ym)
-
-        sums.append(total(scaled * v))
+        if j < 3:
+            send(own.at[pl.ds(PAD, X)], hj.at[pl.ds(32, 16)], 1 + j, zm)
+        send(sy.at[j], hj.at[pl.ds(24, 8)], 1 + j, yp)
+        if j < 3:
+            send(sy.at[j], hj.at[pl.ds(56, 8)], 1 + j, ym)
+        send(sx.at[j, pl.ds(8, 8)], hj.at[pl.ds(16, 8)], 1 + j, xp)
+        if j < 3:
+            sx[j, 0:8] = own[pl.ds(PAD, 8, stride=X)]
+            send(sx.at[j, pl.ds(0, 8)], hj.at[pl.ds(48, 8)], 1 + j, xm)
+
+        if j:
+            fold(last[0] * last[5])
+            gradient(j - 1, last[0], *last[2:5])
+        fold(scaled * v)
         z_low = coef[0, X:R] * v[: R - X]
-        z_up = coef[3, 0 : R - X] * v[X:]
         x_low = coef[6] * own[PAD - 1 : PAD - 1 + R]
-        x_up = coef[4] * own[PAD + 1 : PAD + 1 + R]
         y_low = coef[7] * pltpu.roll(v, 1, 1)
-        y_up = coef[5] * pltpu.roll(v, Y - 1, 1)
-        rest = (x_low + x_up) + (y_low + y_up)
-
-        whole(hj, 1 + j).wait_recv()
-        z_low = jnp.concatenate([edge_z[0:X] * hj[0:16], z_low], axis=0)
-        z_up = jnp.concatenate([z_up, edge_z[X : 2 * X] * hj[16:32]], axis=0)
-        x_edge = coef[8] * spread(hj[32:40], hj[40:48])
-        y_edge = coef[9] * unpack_ends(hj[48:56], hj[56:64])
-        image = ((z_low + z_up) + rest) + (x_edge + y_edge)
-        sums.append(total(v * image))
-
-        g0 = coef[0] * v - z_low
-        g1 = coef[1] * v - x_low - jnp.where(in_x == 0, x_edge, 0.0)
-        g2 = coef[2] * v - y_low - jnp.where(lane == 0, y_edge, 0.0)
-        grads[j, 0] = g0
-        grads[j, 1] = g1
-        grads[j, 2] = g2
-        grads[j, 3] = g0 + g1 + g2
-        scaled = image
-
-    folded = jnp.zeros((8, Y), jnp.float32)
-    for m, value in enumerate(sums):
-        value = value + pltpu.roll(value, 64, 1)
-        value = value + pltpu.roll(value, 32, 1)
-        value = value + pltpu.roll(value, 16, 1)
-        folded = jnp.where(lane8 // 16 == m, value, folded)
-    line = jnp.sum(folded, axis=0, keepdims=True)
+        if j < 3:
+            z_up = coef[3, 0 : R - X] * v[X:]
+            x_up = coef[4] * own[PAD + 1 : PAD + 1 + R]
+            y_up = coef[5] * pltpu.roll(v, Y - 1, 1)
+            rest = (x_low + x_up) + (y_low + y_up)
+        if j == 1:
+            scatter([vel_sum, grads.at[0, 3]], send_a, recv_a, 8, FAR_FIRST[1:])
+        if j == 2:
+            hand_out(send_a, recv_a, 8, FAR_FIRST[:1])
+            scatter([grads.at[1, 3]], send_b, recv_b, 9, FAR_FIRST)
+
+        if j < 3:
+            whole(hj, 1 + j).wait_recv()
+            z_low = jnp.concatenate([edge_z[0:X] * hj[0:16], z_low], axis=0)
+            z_up = jnp.concatenate([z_up, edge_z[X : 2 * X] * hj[32:48]], axis=0)
+            x_edge = coef[8] * spread(hj[16:24], hj[48:56])
+            y_edge = coef[9] * unpack_ends(hj[24:32], hj[56:64])
+            image = ((z_low + z_up) + rest) + (x_edge + y_edge)
+            x_low = x_low + jnp.where(in_x == 0, x_edge, 0.0)
+            y_low = y_low + jnp.where(lane == 0, y_edge, 0.0)
+            last = (v, None, z_low, x_low, y_low, image)
+            scaled = image
+        else:
+            whole(hj.at[pl.ds(0, 32)], 1 + j).wait_recv()
+            z_low = jnp.concatenate([edge_z[0:X] * hj[0:16], z_low], axis=0)
+            x_edge = coef[8] * spread(hj[16:24], hj[16:24])
+            y_edge = coef[9] * unpack_ends(hj[24:32], hj[24:32])
+            x_low = x_low + jnp.where(in_x == 0, x_edge, 0.0)
+            y_low = y_low + jnp.where(lane == 0, y_edge, 0.0)
+            fold((2.0 * v) * ((z_low + x_low) + y_low))
+
+    line = jnp.sum(folded[-1], axis=0, keepdims=True)
     for stage, (name, here, count) in enumerate((("gx", ix, nx), ("gy", iy, ny), ("gz", iz, nz))):
         row_send[stage] = line
         for k in FAR_FIRST:
@@ -273,6 +319,14 @@
                     5 + stage,
                     {name: lax.rem(here + k, count)},
                 )
+        if stage == 0:
+            gradient(3, v, z_low, x_low, y_low)
+            scatter([grads.at[2, 3], grads.at[3, 3]], send_c, recv_c, 10, FAR_FIRST)
+        if stage == 2:
+            for ref, group_id in ((recv_a, 8), (recv_b, 9), (recv_c, 10)):
+                whole(ref.at[pl.ds(0, ref.shape[0] // nz * (nz - 1))], group_id).wait_recv()
+            for copy in params:
+                copy.wait()
         whole(row_recv.at[stage, pl.ds(0, count - 1)], 5 + stage).wait_recv()
         for k in range(count - 1):
             line = line + row_recv[stage, k]
@@ -297,35 +351,24 @@
             value = value - a[p][j] * c[j]
         c[p] = value * pivots[p]
 
-    vel = [vel_v[d * R : (d + 1) * R] for d in range(3)]
-    scalar = vel[0] + vel[1] + vel[2]
-    for j in range(4):
-        scalar = scalar - c[j] * grads[j, 3]
-    scal_v[...] = scalar
-    for t in range(TF):
-        scal_send[t, 0:8] = scal_v[pl.ds(t, 8, stride=8)]
-        scal_send[t, 8:16] = scal_v[pl.ds(R // 2 + t, 8, stride=8)]
-    for k in FAR_FIRST:
-        to = lax.rem(iz + k, nz)
-        send(scal_send.at[to], scal_recv.at[pl.ds(iz * 16, 16)], 8, {"gz": to})
-    scal_recv[pl.ds(pl.multiple_of(iz * 16, 16), 16)] = scal_send[iz]
-    for d in range(3):
-        value = vel[d]
-        for j in range(4):
-            value = value - c[j] * grads[j, d]
-        corrected[d * R : (d + 1) * R] = value
-    whole(scal_recv.at[pl.ds(0, 16 * (nz - 1))], 8).wait_recv()
-
-    field = [
-        jnp.concatenate([scal_recv[pl.ds(2 * z + r, 8, stride=16)] for r in range(2)], axis=0)
-        for z in range(Z)
-    ]
+    field = []
+    for z in range(Z):
+        halves = []
+        for r in range(2):
+            at = 2 * z + r
+            value = recv_a[pl.ds(at, 8, stride=32)]
+            value = value - c[0] * recv_a[pl.ds(16 + at, 8, stride=32)]
+            value = value - c[1] * recv_b[pl.ds(at, 8, stride=16)]
+            value = value - c[2] * recv_c[pl.ds(at, 8, stride=32)]
+            value = value - c[3] * recv_c[pl.ds(16 + at, 8, stride=32)]
+            halves.append(value)
+        field.append(jnp.concatenate(halves, axis=0))
     sub = lax.broadcasted_iota(jnp.int32, (8, Y), 0)
     for k in FAR_FIRST + (0,):
         t = lax.rem(iz + k, nz)
         half = 0.5 / (Z * nz) * gain[t]
-        slopes = [0.5 * slope[t, i] for i in range(4)]
-        offsets = [0.5 * offset[t, i] for i in range(4)]
+        slopes = [0.5 * slope[i, t] for i in range(4)]
+        offsets = [0.5 * offset[i, t] for i in range(4)]
         through = jnp.ones((16, Y), jnp.float32)
         colors = [jnp.zeros((16, Y), jnp.float32) for _ in range(3)]
         for z in range(Z):
@@ -346,27 +389,31 @@
         tile = jnp.concatenate([lines[i][r] for i in range(4) for r in range(2)], axis=0)
         if k:
             img_send[t] = tile
-            send(img_send.at[t], img_recv.at[pl.ds(iz * 8, 8)], 9, {"gz": t})
+            send(img_send.at[t], img_recv.at[pl.ds(iz * 8, 8)], 11, {"gz": t})
         else:
             img_recv[pl.ds(pl.multiple_of(iz * 8, 8), 8)] = tile
-    whole(img_recv.at[pl.ds(0, 8 * (nz - 1))], 9).wait_recv()
+    for d in range(3):
+        value = vel_v[d * R : (d + 1) * R]
+        for j in range(4):
+            value = value - c[j] * grads[j, d]
+        corrected[d * R : (d + 1) * R] = value
+    whole(img_recv.at[pl.ds(0, 8 * (nz - 1))], 11).wait_recv()
     for i in range(4):
         for r in range(2):
             images[i * X + 8 * r : i * X + 8 * r + 8] = img_recv[pl.ds(2 * i + r, 8, stride=8)]
 
     whole(h1, 0).wait_send()
     for j in range(4):
-        whole(h.at[j], 1 + j).wait_send()
+        whole(h.at[j, pl.ds(0, 64 if j < 3 else 32)], 1 + j).wait_send()
     for stage, count in enumerate((nx, ny, nz)):
         whole(row_recv.at[stage, pl.ds(0, count - 1)], 5 + stage).wait_send()
-    whole(scal_recv.at[pl.ds(0, 16 * (nz - 1))], 8).wait_send()
-    whole(img_recv.at[pl.ds(0, 8 * (nz - 1))], 9).wait_send()
+    for ref, group_id in ((recv_a, 8), (recv_b, 9), (recv_c, 10), (img_recv, 11)):
+        whole(ref.at[pl.ds(0, ref.shape[0] // nz * (nz - 1))], group_id).wait_send()
 
 
 def local(sizes, phase_field, thermal, velocity, transfer_slope, transfer_offset, transfer_gain):
     f32 = jnp.float32
-    hbm = pl.BlockSpec(memory_space=pl.ANY)
-    smem = pl.BlockSpec(memory_space=pltpu.SMEM)
+    hbm = pl.BlockSpec(memory_space=pltpu.HBM)
     vmem = pl.BlockSpec(memory_space=pltpu.VMEM)
     corrected, images = pl.pallas_call(
         functools.partial(kernel, sizes),
@@ -374,9 +421,12 @@
             jax.ShapeDtypeStruct((3 * R, Y), f32),
             jax.ShapeDtypeStruct((4 * X, Y), f32),
         ),
-        in_specs=[hbm, hbm, hbm, smem, smem, smem],
+        in_specs=[hbm] * 6,
         out_specs=(vmem, vmem),
         scratch_shapes=[
+            pltpu.SMEM((4, TF), f32),
+            pltpu.SMEM((4, TF), f32),
+            pltpu.SMEM((TF,), f32),
             pltpu.VMEM((R, Y), jnp.int32),
             pltpu.VMEM((R, Y), f32),
             pltpu.VMEM((3 * R, Y), f32),
@@ -396,24 +446,28 @@
             pltpu.VMEM((4, 4, R, Y), f32),
             pltpu.VMEM((3, 1, Y), f32),
             pltpu.VMEM((3, 7, 1, Y), f32),
+            pltpu.VMEM((TF, 32, Y), f32),
+            pltpu.VMEM((TF, 16, Y), f32),
+            pltpu.VMEM((TF, 32, Y), f32),
+            pltpu.VMEM((TF * 32, Y), f32),
+            pltpu.VMEM((TF * 16, Y), f32),
+            pltpu.VMEM((TF * 32, Y), f32),
             pltpu.VMEM((R, Y), f32),
-            pltpu.VMEM((TF, 16, Y), f32),
-            pltpu.VMEM((TF * 16, Y), f32),
             pltpu.VMEM((TF, 8, Y), f32),
             pltpu.VMEM((TF * 8, Y), f32),
-            pltpu.SemaphoreType.DMA((3,)),
-            pltpu.SemaphoreType.DMA((10,)),
-            pltpu.SemaphoreType.DMA((10,)),
+            pltpu.SemaphoreType.DMA((6,)),
+            pltpu.SemaphoreType.DMA((12,)),
+            pltpu.SemaphoreType.DMA((12,)),
         ],
         compiler_params=pltpu.CompilerParams(
-            collective_id=0, has_side_effects=True, vmem_limit_bytes=16 * 2**20
+            collective_id=0, has_side_effects=True, vmem_limit_bytes=64000 * 1024
         ),
     )(
         phase_field.reshape(R, Y),
         thermal.reshape(R, Y),
         velocity.reshape(3 * R, Y),
-        transfer_slope,
-        transfer_offset,
+        transfer_slope.T,
+        transfer_offset.T,
         transfer_gain,
     )
     return corrected.reshape(3, Z, X, Y), images.reshape(1, 4, X, Y)

time: 62.2 us -> 50.5 us (0.81)
  Pallas kernels: 55.4 us -> 47.4 us
  local copies, waits for them, and re-layouts: 5.91 us -> 2.24 us
    pallas_call x1, Pallas kernels: 55.4 us -> 47.4 us  [local(): pl.pallas_call(functools.partial(kernel, sizes), out_shape=(jax.ShapeDtyp...]
    unnamed x16 -> x4, local copies, waits for them, and re-layouts: 5.91 us -> 2.24 us
where the time goes in v2:
time: 50.5 us; the launch traced here: 50.3 us
  Pallas kernels  47.4 us (94%)
  local copies, waits for them, and re-layouts  2.24 us (4%)
  between operations  0.65 us (1%)
    pallas_call x1, Pallas kernels, local(): pl.pallas_call(functools.partial(kernel, sizes), out_shape=(jax.ShapeDtyp...  47.4 us
    unnamed x4, local copies, waits for them, and re-layouts  2.24 us

profile of v2, /device:TPU:8, one launch (start us, length us, event | category | flops | bytes accessed | tf_op | source)
XLA Modules:
  0.0 50.3 jit_solution(2588820407840621428)
XLA Ops:
  0.6 47.4 %shard_map.77 = (f32[384,128]{1,0:T(8,128)}, f32[64,128]{1,0:T(8,128)}) custom-call(s32[128,128]{1,0:T(8,128)} %bitcast.9, f32[128,128]{1,0:T(8,128)} %bitcast.10, f32[384,128]{1,0:T(8,128)} %bitcast.8, f32[4,8]{1,0:T(4,128)} %bitcast.12, f32[4,8]{1,0:T(4,128)} %bitcast.13, f32[8]{0:T(128)} %gain_in.1), custom_call_target="tpu_custom_call" | custom-call | tf_op jit(solution)/shard_map/pallas_call | solution.py:418
  48.0 0.0 copy-start
  48.1 1.6 %copy.10 = f32[3,8,16,128]{3,2,1,0:T(8,128)} copy(f32[3,8,16,128]{3,2,1,0:T(8,128)} %bitcast.7) | data formatting | bytes 393216
  49.7 0.0 copy-done
  49.7 0.6 %copy.11 = f32[1,4,16,128]{3,2,1,0:T(8,128)} copy(f32[1,4,16,128]{3,2,1,0:T(8,128)S(1)} %bitcast.11) | data formatting | bytes 65536
Async XLA Ops:
  48.0 1.6 %copy-start = (f32[64,128]{1,0:T(8,128)S(1)}, f32[64,128]{1,0:T(8,128)}, u32[]{:S(2)}) copy-start(f32[64,128]{1,0:T(8,128)} %get-tuple-element.5) | copy-start | bytes 98308

commit v3 on v2

--- a/solution.py
+++ b/solution.py
@@ -83,7 +83,8 @@
     h,
     grads,
     row_send,
-    row_recv,
+    row_plane,
+    row_line,
     send_a,
     send_b,
     send_c,
@@ -96,6 +97,7 @@
     in_sem,
     send_sem,
     recv_sem,
+    known,
 ):
     nx, ny, nz = sizes
     ix, iy, iz = lax.axis_index("gx"), lax.axis_index("gy"), lax.axis_index("gz")
@@ -135,6 +137,14 @@
     def whole(ref, group_id):
         return pltpu.make_async_remote_copy(
             ref, ref, send_sem.at[group_id], recv_sem.at[group_id], device_id=xp, device_id_type=MESH
+        )
+
+    def in_plane(dx, dy):
+        return {"gx": lax.rem(ix + dx, nx), "gy": lax.rem(iy + dy, ny)}
+
+    def hello(which, dx, dy):
+        pl.semaphore_signal(
+            known.at[which], inc=1, device_id=in_plane(dx, dy), device_id_type=MESH
         )
 
     lane = lanes((R, Y))
@@ -167,6 +177,10 @@
     send(s1y, h1.at[pl.ds(72, 8)], 0, yp)
     send(s1y, h1.at[pl.ds(80, 8)], 0, ym)
     whole(h1, 0).wait_recv()
+    wide = nx == 8 and ny == 8
+    if wide:
+        for dx, dy in ((2, 0), (6, 0), (0, 2), (0, 6)):
+            hello(0, dx, dy)
 
     def face(first, own, other):
         return jnp.where(first, own, other)
@@ -289,6 +303,12 @@
             scatter([grads.at[1, 3]], send_b, recv_b, 9, FAR_FIRST)
 
         if j < 3:
+            if wide and j == 1:
+                pl.semaphore_wait(known.at[0], 4)
+                hello(1, 4, 0)
+                hello(1, 0, 4)
+            if wide and j == 2:
+                pl.semaphore_wait(known.at[1], 2)
             whole(hj, 1 + j).wait_recv()
             z_low = jnp.concatenate([edge_z[0:X] * hj[0:16], z_low], axis=0)
             z_up = jnp.concatenate([z_up, edge_z[X : 2 * X] * hj[32:48]], axis=0)
@@ -309,27 +329,31 @@
             fold((2.0 * v) * ((z_low + x_low) + y_low))
 
     line = jnp.sum(folded[-1], axis=0, keepdims=True)
-    for stage, (name, here, count) in enumerate((("gx", ix, nx), ("gy", iy, ny), ("gz", iz, nz))):
-        row_send[stage] = line
-        for k in FAR_FIRST:
-            if k < count:
-                send(
-                    row_send.at[stage],
-                    row_recv.at[stage, k - 1],
-                    5 + stage,
-                    {name: lax.rem(here + k, count)},
-                )
-        if stage == 0:
-            gradient(3, v, z_low, x_low, y_low)
-            scatter([grads.at[2, 3], grads.at[3, 3]], send_c, recv_c, 10, FAR_FIRST)
-        if stage == 2:
-            for ref, group_id in ((recv_a, 8), (recv_b, 9), (recv_c, 10)):
-                whole(ref.at[pl.ds(0, ref.shape[0] // nz * (nz - 1))], group_id).wait_recv()
-            for copy in params:
-                copy.wait()
-        whole(row_recv.at[stage, pl.ds(0, count - 1)], 5 + stage).wait_recv()
-        for k in range(count - 1):
-            line = line + row_recv[stage, k]
+    row_send[0] = line
+    others = [(dx, dy) for dx in range(nx) for dy in range(ny) if dx or dy]
+
+    def hops(apart):
+        dx, dy = apart
+        return min(dx, nx - dx) / 2 + min(dy, ny - dy)
+
+    others.sort(key=hops, reverse=True)
+    for at, apart in enumerate(others):
+        send(row_send.at[0], row_plane.at[pl.ds(at, 1)], 5, in_plane(*apart))
+    row_plane[pl.ds(len(others), 1)] = line
+    gradient(3, v, z_low, x_low, y_low)
+    scatter([grads.at[2, 3], grads.at[3, 3]], send_c, recv_c, 10, FAR_FIRST)
+    whole(row_plane.at[pl.ds(0, len(others))], 5).wait_recv()
+    line = jnp.sum(row_plane[0 : len(others) + 1], axis=0, keepdims=True)
+    row_send[1] = line
+    for k in FAR_FIRST:
+        send(row_send.at[1], row_line.at[pl.ds(k - 1, 1)], 6, {"gz": lax.rem(iz + k, nz)})
+    row_line[nz - 1 : nz] = line
+    for ref, group_id in ((recv_a, 8), (recv_b, 9), (recv_c, 10)):
+        whole(ref.at[pl.ds(0, ref.shape[0] // nz * (nz - 1))], group_id).wait_recv()
+    for copy in params:
+        copy.wait()
+    whole(row_line.at[pl.ds(0, nz - 1)], 6).wait_recv()
+    line = jnp.sum(row_line[...], axis=0, keepdims=True)
     lane1 = lanes((1, Y))
     m = [jnp.sum(jnp.where(lane1 // 16 == i, line, 0.0), axis=1, keepdims=True) for i in range(8)]
 
@@ -405,8 +429,8 @@
     whole(h1, 0).wait_send()
     for j in range(4):
         whole(h.at[j, pl.ds(0, 64 if j < 3 else 32)], 1 + j).wait_send()
-    for stage, count in enumerate((nx, ny, nz)):
-        whole(row_recv.at[stage, pl.ds(0, count - 1)], 5 + stage).wait_send()
+    whole(row_plane.at[pl.ds(0, len(others))], 5).wait_send()
+    whole(row_line.at[pl.ds(0, nz - 1)], 6).wait_send()
     for ref, group_id in ((recv_a, 8), (recv_b, 9), (recv_c, 10), (img_recv, 11)):
         whole(ref.at[pl.ds(0, ref.shape[0] // nz * (nz - 1))], group_id).wait_send()
 
@@ -444,8 +468,9 @@
             pltpu.VMEM((4, 8, Y), f32),
             pltpu.VMEM((4, 64, Y), f32),
             pltpu.VMEM((4, 4, R, Y), f32),
-            pltpu.VMEM((3, 1, Y), f32),
-            pltpu.VMEM((3, 7, 1, Y), f32),
+            pltpu.VMEM((2, 1, Y), f32),
+            pltpu.VMEM((sizes[0] * sizes[1], Y), f32),
+            pltpu.VMEM((sizes[2], Y), f32),
             pltpu.VMEM((TF, 32, Y), f32),
             pltpu.VMEM((TF, 16, Y), f32),
             pltpu.VMEM((TF, 32, Y), f32),
@@ -458,17 +483,23 @@
             pltpu.SemaphoreType.DMA((6,)),
             pltpu.SemaphoreType.DMA((12,)),
             pltpu.SemaphoreType.DMA((12,)),
+            pltpu.SemaphoreType.REGULAR((2,)),
         ],
         compiler_params=pltpu.CompilerParams(
-            collective_id=0, has_side_effects=True, vmem_limit_bytes=64000 * 1024
+            collective_id=0, has_side_effects=True, vmem_limit_bytes=16 * 2**20
         ),
     )(
-        phase_field.reshape(R, Y),
-        thermal.reshape(R, Y),
-        velocity.reshape(3 * R, Y),
-        transfer_slope.T,
-        transfer_offset.T,
-        transfer_gain,
+        *(
+            pltpu.with_memory_space_constraint(value, pltpu.HBM)
+            for value in (
+                phase_field.reshape(R, Y),
+                thermal.reshape(R, Y),
+                velocity.reshape(3 * R, Y),
+                transfer_slope.T,
+                transfer_offset.T,
+                transfer_gain,
+            )
+        )
     )
     return corrected.reshape(3, Z, X, Y), images.reshape(1, 4, X, Y)
 

time: 50.5 us -> 46.7 us (0.925)
  Pallas kernels: 47.4 us -> 44.7 us
  local copies, waits for them, and re-layouts: 2.24 us -> 1.29 us
    pallas_call x1, Pallas kernels: 47.4 us -> 44.7 us  [local(): pl.pallas_call(functools.partial(kernel, sizes), out_shape=(jax.ShapeDtyp...]
    unnamed x4 -> x2, local copies, waits for them, and re-layouts: 2.24 us -> 1.29 us
where the time goes in v3:
time: 46.7 us; the launch traced here: 46.6 us
  Pallas kernels  44.7 us (96%)
  local copies, waits for them, and re-layouts  1.29 us (3%)
  between operations  0.64 us (1%)
    pallas_call x1, Pallas kernels, local(): pl.pallas_call(functools.partial(kernel, sizes), out_shape=(jax.ShapeDtyp...  44.7 us
    unnamed x2, local copies, waits for them, and re-layouts  1.29 us

profile of v3, /device:TPU:8, one launch (start us, length us, event | category | flops | bytes accessed | tf_op | source)
XLA Modules:
  0.0 46.6 jit_solution(4564612351594980596)
XLA Ops:
  0.6 44.7 %shard_map.77 = (f32[384,128]{1,0:T(8,128)S(1)}, f32[64,128]{1,0:T(8,128)S(1)}) custom-call(s32[128,128]{1,0:T(8,128)} %bitcast.10, f32[128,128]{1,0:T(8,128)} %bitcast.11, f32[384,128]{1,0:T(8,128)} %bitcast.9, f32[4,8]{1,0:T(4,128)} %bitcast.12, f32[4,8]{1,0:T(4,128)} %bitcast.13, f32[8]{0:T(128)} %gain_in.1), custom_call_target="tpu_custom_call" | custom-call | tf_op jit(solution)/shard_map/pallas_call | solution.py:442
  45.3 0.7 %copy.10 = f32[3,8,16,128]{3,2,1,0:T(8,128)} copy(f32[3,8,16,128]{3,2,1,0:T(8,128)S(1)} %bitcast.7) | data formatting | bytes 393216
  46.0 0.6 %copy.11 = f32[1,4,16,128]{3,2,1,0:T(8,128)} copy(f32[1,4,16,128]{3,2,1,0:T(8,128)S(1)} %bitcast.8) | data formatting | bytes 65536

commit v4 on v3

--- a/solution.py
+++ b/solution.py
@@ -38,10 +38,19 @@
     return out
 
 
-def unpack_ends(below, above):
-    lane = lanes((8, Y))
-    both = jnp.where(lane % 2 == 0, pltpu.roll(above, Y - 1, 1), pltpu.roll(below, 1, 1))
+def merge(below, above):
+    even = lanes((8, Y)) % 2 == 0
+    return jnp.where(even, pltpu.roll(above, Y - 1, 1), pltpu.roll(below, 1, 1))
+
+
+def unpack(both):
     return jnp.concatenate([pltpu.roll(both, Y - (2 * k + 1), 1) for k in range(K)], axis=0)
+
+
+def rows_of(first, second):
+    return jnp.concatenate(
+        [jnp.broadcast_to(first, (8, Y)), jnp.broadcast_to(second, (8, Y))], axis=0
+    )
 
 
 def spread(below, above):
@@ -78,18 +87,24 @@
     v_pad,
     coef,
     edge_z,
-    sx,
-    sy,
+    weights,
+    stat_z,
+    stat_x,
+    stat_y,
+    stat,
+    stat_m,
+    scaled_v,
+    dz,
+    dx,
+    dy,
     h,
     grads,
     row_send,
     row_plane,
     row_line,
     send_a,
-    send_b,
     send_c,
     recv_a,
-    recv_b,
     recv_c,
     vel_sum,
     img_send,
@@ -179,8 +194,12 @@
     whole(h1, 0).wait_recv()
     wide = nx == 8 and ny == 8
     if wide:
-        for dx, dy in ((2, 0), (6, 0), (0, 2), (0, 6)):
-            hello(0, dx, dy)
+        for far in ((2, 0), (6, 0), (0, 2), (0, 6)):
+            hello(0, *far)
+    for step in (2, 6):
+        pl.semaphore_signal(
+            known.at[2], inc=1, device_id={"gz": lax.rem(iz + step, nz)}, device_id_type=MESH
+        )
 
     def face(first, own, other):
         return jnp.where(first, own, other)
@@ -190,7 +209,7 @@
     bx = spread(h1[48:56], h1[56:64])
     xb = jnp.where(in_x == 0, face(x_first, den, bx), den_pad[PAD - 1 : PAD - 1 + R])
     xa = jnp.where(in_x == X - 1, face(x_last, den, bx), den_pad[PAD + 1 : PAD + 1 + R])
-    by = unpack_ends(h1[72:80], h1[80:88])
+    by = unpack(merge(h1[72:80], h1[80:88]))
     yb = jnp.where(lane == 0, face(y_first, den, by), pltpu.roll(den, 1, 1))
     ya = jnp.where(lane == Y - 1, face(y_last, den, by), pltpu.roll(den, Y - 1, 1))
     low_z, up_z = 2.0 * recip(den + zb), 2.0 * recip(den + za)
@@ -220,6 +239,25 @@
     edge_z[0:X] = low_z[0:X] * keep(z_first)
     edge_z[X : 2 * X] = up_z[R - X :] * keep(z_last)
 
+    weights[0] = inverse * coef[8]
+    weights[1] = inverse * coef[9]
+    weights[2] = zero
+    weights[2, 0:X] = inverse[0:X] * edge_z[0:X]
+    weights[2, R - X : R] = inverse[R - X :] * edge_z[X : 2 * X]
+    for i in range(3):
+        stat_z[0, 16 * i : 16 * i + 16] = weights[i, 0:X]
+        stat_z[1, 16 * i : 16 * i + 16] = weights[i, R - X : R]
+        face_x = weights.at[i]
+        stat_x[0, 8 * i : 8 * i + 8] = face_x[pl.ds(0, 8, stride=X)]
+        stat_x[1, 8 * i : 8 * i + 8] = face_x[pl.ds(X - 1, 8, stride=X)]
+        stat_y[8 * i : 8 * i + 8] = pack_ends(weights[i])
+    send(stat_z.at[1], stat.at[pl.ds(0, 48)], 3, zp)
+    send(stat_z.at[0], stat.at[pl.ds(48, 48)], 3, zm)
+    send(stat_y, stat.at[pl.ds(96, 24)], 3, yp)
+    send(stat_y, stat.at[pl.ds(120, 24)], 3, ym)
+    send(stat_x.at[1], stat.at[pl.ds(144, 24)], 3, xp)
+    send(stat_x.at[0], stat.at[pl.ds(168, 24)], 3, xm)
+
     above0 = jnp.concatenate([vel0[X:], h1[32:48] * keep(z_last)], axis=0)
     bv = spread(h1[56:64], h1[64:72])
     above1 = jnp.where(in_x == X - 1, bv * keep(x_last), vel1_pad[PAD + 1 : PAD + 1 + R])
@@ -263,31 +301,99 @@
         grads[j, 2] = g2
         grads[j, 3] = g0 + g1 + g2
 
+    def near(axis, here, count, step):
+        return {axis: lax.rem(here + count - step, count)}
+
+    def exchange(p, own, v, inner):
+        nxt = coef[10] * inner
+        scaled_v[p] = nxt
+        hp = h.at[p]
+        for side, at in ((1, R - X), (0, 0)):
+            dz[p, side, 0:16] = v[at : at + X]
+            dz[p, side, 16:32] = nxt[at : at + X]
+        q = pack_ends(v)
+        dy[p, 0:8] = q
+        dy[p, 8:16] = pack_ends(nxt)
+        for side, at in ((1, X - 1), (0, 0)):
+            dx[p, side, 0:8] = scaled_v.at[p][pl.ds(at, 8, stride=X)]
+            dx[p, side, 8:16] = own[pl.ds(PAD + at, 8, stride=X)]
+            dx[p, side, 16:24] = q
+        signs = ((-1, -1), (-1, 1), (1, -1), (1, 1))
+        for i, (a, b) in enumerate(signs):
+            row_at = PAD + (R - X if a < 0 else 0) + (X - 1 if b < 0 else 0)
+            to = near("gz", iz, nz, a) | near("gx", ix, nx, b)
+            send(own.at[pl.ds(row_at, 1)], hp.at[pl.ds(224 + i, 1)], 1 + p, to)
+        for i, (a, b) in enumerate(signs):
+            to = near("gz", iz, nz, a) | near("gy", iy, ny, b)
+            send(dy.at[p, pl.ds(0, 8)], hp.at[pl.ds(128 + 8 * i, 8)], 1 + p, to)
+        for i, (a, b) in enumerate(signs):
+            to = near("gx", ix, nx, a) | near("gy", iy, ny, b)
+            side = 1 if a < 0 else 0
+            send(dx.at[p, side, pl.ds(8, 16)], hp.at[pl.ds(160 + 16 * i, 16)], 1 + p, to)
+        send(dz.at[p, 1], hp.at[pl.ds(0, 32)], 1 + p, zp)
+        send(dz.at[p, 0], hp.at[pl.ds(32, 32)], 1 + p, zm)
+        send(dy.at[p], hp.at[pl.ds(96, 16)], 1 + p, yp)
+        send(dy.at[p], hp.at[pl.ds(112, 16)], 1 + p, ym)
+        send(dx.at[p, 1, pl.ds(0, 16)], hp.at[pl.ds(64, 16)], 1 + p, xp)
+        send(dx.at[p, 0, pl.ds(0, 16)], hp.at[pl.ds(80, 16)], 1 + p, xm)
+
+    sub8 = lax.broadcasted_iota(jnp.int32, (8, Y), 0)
+
+    def received(p):
+        hp = h.at[p]
+        z_faces = (hp[0:16], hp[32:48])
+        x_faces = (hp[72:80], hp[88:96])
+        return z_faces, x_faces, merge(hp[96:104], hp[112:120])
+
+    def computed(p, v):
+        hp = h.at[p]
+        corner = [[hp[224 + 2 * a + b : 225 + 2 * a + b] for b in range(2)] for a in range(2)]
+        zy = [merge(hp[128 + 16 * a : 136 + 16 * a], hp[136 + 16 * a : 144 + 16 * a]) for a in (0, 1)]
+        xy_rows = [[hp[160 + 32 * a + 16 * b : 168 + 32 * a + 16 * b] for b in (0, 1)] for a in (0, 1)]
+        xy = [merge(hp[168 + 32 * a : 176 + 32 * a], hp[184 + 32 * a : 192 + 32 * a]) for a in (0, 1)]
+        z_faces, x_faces = [], []
+        for a, (at, first) in enumerate(((0, 2 * K - 4), (R - X, 0))):
+            from_y = jnp.concatenate(
+                [pltpu.roll(zy[a], Y - first - 1, 1), pltpu.roll(zy[a], Y - first - 3, 1)], axis=0
+            )
+            value = hp[16 + 32 * a : 32 + 32 * a]
+            value = value + stat[48 * a + 32 : 48 * a + 48] * v[at : at + X]
+            value = value + stat[48 * a : 48 * a + 16] * rows_of(corner[a][0], corner[a][1])
+            z_faces.append(value + stat[48 * a + 16 : 48 * a + 32] * from_y)
+        for a in range(2):
+            mine = dx[p, a, 8:16]
+            from_z = jnp.where(
+                sub8 == 0,
+                jnp.broadcast_to(corner[0][a], (8, Y)),
+                jnp.broadcast_to(corner[1][a], (8, Y)),
+            )
+            from_y = jnp.where(
+                lane8 == 0, pltpu.roll(xy_rows[a][0], 1, 1), pltpu.roll(xy_rows[a][1], Y - 1, 1)
+            )
+            at = 144 + 24 * a
+            value = hp[64 + 16 * a : 72 + 16 * a] + stat[at : at + 8] * mine
+            value = value + stat[at + 8 : at + 16] * from_y
+            x_faces.append(value + stat[at + 16 : at + 24] * from_z)
+        last_z = 2 * K - 4
+        from_z = jnp.where(lane8 < 4, pltpu.roll(zy[0], Y - last_z, 1), pltpu.roll(zy[1], last_z, 1))
+        from_x = jnp.where(
+            sub8 == 0,
+            pltpu.roll(pltpu.roll(xy[0], Y - 2, 1), 1, 0),
+            pltpu.roll(pltpu.roll(xy[1], 2, 1), 7, 0),
+        )
+        both = merge(hp[104:112], hp[120:128])
+        both = both + stat_m[8:16] * dy[p, 0:8]
+        both = both + stat_m[0:8] * from_x
+        return z_faces, x_faces, both + stat_m[16:24] * from_z
+
     vel_sum[...] = vel0 + vel1 + vel2
     scaled = rhs
-    last = None
+    late = None
     for j in range(4):
+        p = j // 2
         v = coef[10] * scaled
         own = v_pad.at[j]
         own[PAD : PAD + R] = v
-        sx[j, 8:16] = own[pl.ds(PAD + X - 1, 8, stride=X)]
-        sy[j] = pack_ends(v)
-        hj = h.at[j]
-        send(own.at[pl.ds(PAD + R - X, X)], hj.at[pl.ds(0, 16)], 1 + j, zp)
-        if j < 3:
-            send(own.at[pl.ds(PAD, X)], hj.at[pl.ds(32, 16)], 1 + j, zm)
-        send(sy.at[j], hj.at[pl.ds(24, 8)], 1 + j, yp)
-        if j < 3:
-            send(sy.at[j], hj.at[pl.ds(56, 8)], 1 + j, ym)
-        send(sx.at[j, pl.ds(8, 8)], hj.at[pl.ds(16, 8)], 1 + j, xp)
-        if j < 3:
-            sx[j, 0:8] = own[pl.ds(PAD, 8, stride=X)]
-            send(sx.at[j, pl.ds(0, 8)], hj.at[pl.ds(48, 8)], 1 + j, xm)
-
-        if j:
-            fold(last[0] * last[5])
-            gradient(j - 1, last[0], *last[2:5])
-        fold(scaled * v)
         z_low = coef[0, X:R] * v[: R - X]
         x_low = coef[6] * own[PAD - 1 : PAD - 1 + R]
         y_low = coef[7] * pltpu.roll(v, 1, 1)
@@ -296,36 +402,51 @@
             x_up = coef[4] * own[PAD + 1 : PAD + 1 + R]
             y_up = coef[5] * pltpu.roll(v, Y - 1, 1)
             rest = (x_low + x_up) + (y_low + y_up)
-        if j == 1:
-            scatter([vel_sum, grads.at[0, 3]], send_a, recv_a, 8, FAR_FIRST[1:])
-        if j == 2:
-            hand_out(send_a, recv_a, 8, FAR_FIRST[:1])
-            scatter([grads.at[1, 3]], send_b, recv_b, 9, FAR_FIRST)
-
-        if j < 3:
-            if wide and j == 1:
-                pl.semaphore_wait(known.at[0], 4)
+        if j % 2 == 0:
+            edge = jnp.zeros((X, Y), jnp.float32)
+            inner = jnp.concatenate([edge, z_low], axis=0) + jnp.concatenate([z_up, edge], axis=0)
+            exchange(p, own, v, inner + rest)
+            earlier = late
+            if j:
+                fold(last[0] * last[4])
+                gradient(*earlier)
+                gradient(1, *last[:4])
+                scatter([vel_sum, grads.at[0, 3], grads.at[1, 3]], send_a, recv_a, 8, FAR_FIRST)
+            fold(scaled * v)
+            if j == 0:
+                if wide:
+                    pl.semaphore_wait(known.at[0], 4)
+                pl.semaphore_wait(known.at[2], 2)
+                whole(stat, 3).wait_recv()
+                for i in range(3):
+                    stat_m[8 * i : 8 * i + 8] = merge(
+                        stat[96 + 8 * i : 104 + 8 * i], stat[120 + 8 * i : 128 + 8 * i]
+                    )
+            elif wide:
+                pl.semaphore_wait(known.at[1], 2)
+            whole(h.at[p, pl.ds(0, 228)], 1 + p).wait_recv()
+            if wide and j == 0:
                 hello(1, 4, 0)
                 hello(1, 0, 4)
-            if wide and j == 2:
-                pl.semaphore_wait(known.at[1], 2)
-            whole(hj, 1 + j).wait_recv()
-            z_low = jnp.concatenate([edge_z[0:X] * hj[0:16], z_low], axis=0)
-            z_up = jnp.concatenate([z_up, edge_z[X : 2 * X] * hj[32:48]], axis=0)
-            x_edge = coef[8] * spread(hj[16:24], hj[48:56])
-            y_edge = coef[9] * unpack_ends(hj[24:32], hj[56:64])
-            image = ((z_low + z_up) + rest) + (x_edge + y_edge)
-            x_low = x_low + jnp.where(in_x == 0, x_edge, 0.0)
-            y_low = y_low + jnp.where(lane == 0, y_edge, 0.0)
-            last = (v, None, z_low, x_low, y_low, image)
-            scaled = image
+            z_faces, x_faces, both = received(p)
         else:
-            whole(hj.at[pl.ds(0, 32)], 1 + j).wait_recv()
-            z_low = jnp.concatenate([edge_z[0:X] * hj[0:16], z_low], axis=0)
-            x_edge = coef[8] * spread(hj[16:24], hj[16:24])
-            y_edge = coef[9] * unpack_ends(hj[24:32], hj[24:32])
-            x_low = x_low + jnp.where(in_x == 0, x_edge, 0.0)
-            y_low = y_low + jnp.where(lane == 0, y_edge, 0.0)
+            fold(scaled * v)
+            z_faces, x_faces, both = following
+        z_low = jnp.concatenate([edge_z[0:X] * z_faces[0], z_low], axis=0)
+        x_edge = coef[8] * spread(*x_faces)
+        y_edge = coef[9] * unpack(both)
+        x_low = x_low + jnp.where(in_x == 0, x_edge, 0.0)
+        y_low = y_low + jnp.where(lane == 0, y_edge, 0.0)
+        if j < 3:
+            z_up = jnp.concatenate([z_up, edge_z[X : 2 * X] * z_faces[1]], axis=0)
+            scaled = ((z_low + z_up) + rest) + (x_edge + y_edge)
+        if j % 2 == 0:
+            following = computed(p, v)
+            fold(v * scaled)
+            late = (j, v, z_low, x_low, y_low)
+        elif j == 1:
+            last = (v, z_low, x_low, y_low, scaled)
+        else:
             fold((2.0 * v) * ((z_low + x_low) + y_low))
 
     line = jnp.sum(folded[-1], axis=0, keepdims=True)
@@ -340,6 +461,7 @@
     for at, apart in enumerate(others):
         send(row_send.at[0], row_plane.at[pl.ds(at, 1)], 5, in_plane(*apart))
     row_plane[pl.ds(len(others), 1)] = line
+    gradient(*late)
     gradient(3, v, z_low, x_low, y_low)
     scatter([grads.at[2, 3], grads.at[3, 3]], send_c, recv_c, 10, FAR_FIRST)
     whole(row_plane.at[pl.ds(0, len(others))], 5).wait_recv()
@@ -348,7 +470,7 @@
     for k in FAR_FIRST:
         send(row_send.at[1], row_line.at[pl.ds(k - 1, 1)], 6, {"gz": lax.rem(iz + k, nz)})
     row_line[nz - 1 : nz] = line
-    for ref, group_id in ((recv_a, 8), (recv_b, 9), (recv_c, 10)):
+    for ref, group_id in ((recv_a, 8), (recv_c, 10)):
         whole(ref.at[pl.ds(0, ref.shape[0] // nz * (nz - 1))], group_id).wait_recv()
     for copy in params:
         copy.wait()
@@ -380,9 +502,9 @@
         halves = []
         for r in range(2):
             at = 2 * z + r
-            value = recv_a[pl.ds(at, 8, stride=32)]
-            value = value - c[0] * recv_a[pl.ds(16 + at, 8, stride=32)]
-            value = value - c[1] * recv_b[pl.ds(at, 8, stride=16)]
+            value = recv_a[pl.ds(at, 8, stride=48)]
+            value = value - c[0] * recv_a[pl.ds(16 + at, 8, stride=48)]
+            value = value - c[1] * recv_a[pl.ds(32 + at, 8, stride=48)]
             value = value - c[2] * recv_c[pl.ds(at, 8, stride=32)]
             value = value - c[3] * recv_c[pl.ds(16 + at, 8, stride=32)]
             halves.append(value)
@@ -427,11 +549,12 @@
             images[i * X + 8 * r : i * X + 8 * r + 8] = img_recv[pl.ds(2 * i + r, 8, stride=8)]
 
     whole(h1, 0).wait_send()
-    for j in range(4):
-        whole(h.at[j, pl.ds(0, 64 if j < 3 else 32)], 1 + j).wait_send()
+    whole(stat, 3).wait_send()
+    for p in range(2):
+        whole(h.at[p, pl.ds(0, 228)], 1 + p).wait_send()
     whole(row_plane.at[pl.ds(0, len(others))], 5).wait_send()
     whole(row_line.at[pl.ds(0, nz - 1)], 6).wait_send()
-    for ref, group_id in ((recv_a, 8), (recv_b, 9), (recv_c, 10), (img_recv, 11)):
+    for ref, group_id in ((recv_a, 8), (recv_c, 10), (img_recv, 11)):
         whole(ref.at[pl.ds(0, ref.shape[0] // nz * (nz - 1))], group_id).wait_send()
 
 
@@ -464,18 +587,24 @@
             pltpu.VMEM((4, R + 2 * PAD, Y), f32),
             pltpu.VMEM((11, R, Y), f32),
             pltpu.VMEM((2 * X, Y), f32),
-            pltpu.VMEM((4, 16, Y), f32),
-            pltpu.VMEM((4, 8, Y), f32),
-            pltpu.VMEM((4, 64, Y), f32),
+            pltpu.VMEM((3, R, Y), f32),
+            pltpu.VMEM((2, 48, Y), f32),
+            pltpu.VMEM((2, 24, Y), f32),
+            pltpu.VMEM((24, Y), f32),
+            pltpu.VMEM((192, Y), f32),
+            pltpu.VMEM((24, Y), f32),
+            pltpu.VMEM((2, R, Y), f32),
+            pltpu.VMEM((2, 2, 32, Y), f32),
+            pltpu.VMEM((2, 2, 24, Y), f32),
+            pltpu.VMEM((2, 16, Y), f32),
+            pltpu.VMEM((2, 232, Y), f32),
             pltpu.VMEM((4, 4, R, Y), f32),
             pltpu.VMEM((2, 1, Y), f32),
             pltpu.VMEM((sizes[0] * sizes[1], Y), f32),
             pltpu.VMEM((sizes[2], Y), f32),
+            pltpu.VMEM((TF, 48, Y), f32),
             pltpu.VMEM((TF, 32, Y), f32),
-            pltpu.VMEM((TF, 16, Y), f32),
-            pltpu.VMEM((TF, 32, Y), f32),
-            pltpu.VMEM((TF * 32, Y), f32),
-            pltpu.VMEM((TF * 16, Y), f32),
+            pltpu.VMEM((TF * 48, Y), f32),
             pltpu.VMEM((TF * 32, Y), f32),
             pltpu.VMEM((R, Y), f32),
             pltpu.VMEM((TF, 8, Y), f32),
@@ -483,7 +612,7 @@
             pltpu.SemaphoreType.DMA((6,)),
             pltpu.SemaphoreType.DMA((12,)),
             pltpu.SemaphoreType.DMA((12,)),
-            pltpu.SemaphoreType.REGULAR((2,)),
+            pltpu.SemaphoreType.REGULAR((3,)),
         ],
         compiler_params=pltpu.CompilerParams(
             collective_id=0, has_side_effects=True, vmem_limit_bytes=16 * 2**20

time: 46.7 us -> 43.1 us (0.923)
  Pallas kernels: 44.7 us -> 41.1 us
    pallas_call x1, Pallas kernels: 44.7 us -> 41.1 us  [local(): pl.pallas_call(functools.partial(kernel, sizes), out_shape=(jax.ShapeDtyp...]
where the time goes in v4:
time: 43.1 us; the launch traced here: 43 us
  Pallas kernels  41.1 us (95%)
  local copies, waits for them, and re-layouts  1.29 us (3%)
  between operations  0.64 us (1%)
    pallas_call x1, Pallas kernels, local(): pl.pallas_call(functools.partial(kernel, sizes), out_shape=(jax.ShapeDtyp...  41.1 us
    unnamed x2, local copies, waits for them, and re-layouts  1.29 us

profile of v4, /device:TPU:8, one launch (start us, length us, event | category | flops | bytes accessed | tf_op | source)
XLA Modules:
  0.0 43.0 jit_solution(16982584157480751330)
XLA Ops:
  0.6 41.1 %shard_map.77 = (f32[384,128]{1,0:T(8,128)S(1)}, f32[64,128]{1,0:T(8,128)S(1)}) custom-call(s32[128,128]{1,0:T(8,128)} %bitcast.10, f32[128,128]{1,0:T(8,128)} %bitcast.11, f32[384,128]{1,0:T(8,128)} %bitcast.9, f32[4,8]{1,0:T(4,128)} %bitcast.12, f32[4,8]{1,0:T(4,128)} %bitcast.13, f32[8]{0:T(128)} %gain_in.1), custom_call_target="tpu_custom_call" | custom-call | tf_op jit(solution)/shard_map/pallas_call | solution.py:565
  41.7 0.7 %copy.10 = f32[3,8,16,128]{3,2,1,0:T(8,128)} copy(f32[3,8,16,128]{3,2,1,0:T(8,128)S(1)} %bitcast.7) | data formatting | bytes 393216
  42.4 0.6 %copy.11 = f32[1,4,16,128]{3,2,1,0:T(8,128)} copy(f32[1,4,16,128]{3,2,1,0:T(8,128)S(1)} %bitcast.8) | data formatting | bytes 65536

commit v5 on v4

--- a/solution.py
+++ b/solution.py
@@ -133,10 +133,12 @@
         pltpu.make_async_copy(offset_in, offset, in_sem.at[4]),
         pltpu.make_async_copy(gain_in, gain, in_sem.at[5]),
     ]
+    for copy in loads:
+        copy.start()
     barrier = pltpu.get_barrier_semaphore()
     for device in (zm, zp, ym, yp, xm, xp):
         pl.semaphore_signal(barrier, inc=1, device_id=device, device_id_type=MESH)
-    for copy in loads + params:
+    for copy in params:
         copy.start()
 
     pad = jnp.zeros((PAD, Y), jnp.float32)
@@ -304,6 +306,9 @@
     def near(axis, here, count, step):
         return {axis: lax.rem(here + count - step, count)}
 
+    edges = (4, 3)
+    waits = [pl.ds(0, 128 + 25 * count) for count in edges]
+
     def exchange(p, own, v, inner):
         nxt = coef[10] * inner
         scaled_v[p] = nxt
@@ -318,7 +323,7 @@
             dx[p, side, 0:8] = scaled_v.at[p][pl.ds(at, 8, stride=X)]
             dx[p, side, 8:16] = own[pl.ds(PAD + at, 8, stride=X)]
             dx[p, side, 16:24] = q
-        signs = ((-1, -1), (-1, 1), (1, -1), (1, 1))
+        signs = ((-1, -1), (-1, 1), (1, -1), (1, 1))[: edges[p]]
         for i, (a, b) in enumerate(signs):
             row_at = PAD + (R - X if a < 0 else 0) + (X - 1 if b < 0 else 0)
             to = near("gz", iz, nz, a) | near("gx", ix, nx, b)
@@ -347,12 +352,14 @@
 
     def computed(p, v):
         hp = h.at[p]
-        corner = [[hp[224 + 2 * a + b : 225 + 2 * a + b] for b in range(2)] for a in range(2)]
-        zy = [merge(hp[128 + 16 * a : 136 + 16 * a], hp[136 + 16 * a : 144 + 16 * a]) for a in (0, 1)]
-        xy_rows = [[hp[160 + 32 * a + 16 * b : 168 + 32 * a + 16 * b] for b in (0, 1)] for a in (0, 1)]
-        xy = [merge(hp[168 + 32 * a : 176 + 32 * a], hp[184 + 32 * a : 192 + 32 * a]) for a in (0, 1)]
+        low_only = p == 1
+        pairs = ((0, 1), (2, 2 if low_only else 3))
+        corner = [[hp[224 + i : 225 + i] for i in pair] for pair in pairs]
+        zy = [merge(*(hp[128 + 8 * i : 136 + 8 * i] for i in pair)) for pair in pairs]
+        xy_rows = [[hp[160 + 16 * i : 168 + 16 * i] for i in pair] for pair in pairs]
+        xy = [merge(*(hp[168 + 16 * i : 176 + 16 * i] for i in pair)) for pair in pairs]
         z_faces, x_faces = [], []
-        for a, (at, first) in enumerate(((0, 2 * K - 4), (R - X, 0))):
+        for a, (at, first) in enumerate(((0, 2 * K - 4), (R - X, 0))[: 2 - low_only]):
             from_y = jnp.concatenate(
                 [pltpu.roll(zy[a], Y - first - 1, 1), pltpu.roll(zy[a], Y - first - 3, 1)], axis=0
             )
@@ -360,7 +367,7 @@
             value = value + stat[48 * a + 32 : 48 * a + 48] * v[at : at + X]
             value = value + stat[48 * a : 48 * a + 16] * rows_of(corner[a][0], corner[a][1])
             z_faces.append(value + stat[48 * a + 16 : 48 * a + 32] * from_y)
-        for a in range(2):
+        for a in range(2 - low_only):
             mine = dx[p, a, 8:16]
             from_z = jnp.where(
                 sub8 == 0,
@@ -424,7 +431,7 @@
                     )
             elif wide:
                 pl.semaphore_wait(known.at[1], 2)
-            whole(h.at[p, pl.ds(0, 228)], 1 + p).wait_recv()
+            whole(h.at[p, waits[p]], 1 + p).wait_recv()
             if wide and j == 0:
                 hello(1, 4, 0)
                 hello(1, 0, 4)
@@ -433,7 +440,7 @@
             fold(scaled * v)
             z_faces, x_faces, both = following
         z_low = jnp.concatenate([edge_z[0:X] * z_faces[0], z_low], axis=0)
-        x_edge = coef[8] * spread(*x_faces)
+        x_edge = coef[8] * spread(x_faces[0], x_faces[-1])
         y_edge = coef[9] * unpack(both)
         x_low = x_low + jnp.where(in_x == 0, x_edge, 0.0)
         y_low = y_low + jnp.where(lane == 0, y_edge, 0.0)
@@ -453,11 +460,7 @@
     row_send[0] = line
     others = [(dx, dy) for dx in range(nx) for dy in range(ny) if dx or dy]
 
-    def hops(apart):
-        dx, dy = apart
-        return min(dx, nx - dx) / 2 + min(dy, ny - dy)
-
-    others.sort(key=hops, reverse=True)
+    others.sort(key=lambda apart: ((apart[1] - 1) % ny, -min(apart[0], nx - apart[0])))
     for at, apart in enumerate(others):
         send(row_send.at[0], row_plane.at[pl.ds(at, 1)], 5, in_plane(*apart))
     row_plane[pl.ds(len(others), 1)] = line
@@ -551,11 +554,22 @@
     whole(h1, 0).wait_send()
     whole(stat, 3).wait_send()
     for p in range(2):
-        whole(h.at[p, pl.ds(0, 228)], 1 + p).wait_send()
+        whole(h.at[p, waits[p]], 1 + p).wait_send()
     whole(row_plane.at[pl.ds(0, len(others))], 5).wait_send()
     whole(row_line.at[pl.ds(0, nz - 1)], 6).wait_send()
     for ref, group_id in ((recv_a, 8), (recv_c, 10), (img_recv, 11)):
         whole(ref.at[pl.ds(0, ref.shape[0] // nz * (nz - 1))], group_id).wait_send()
+
+
+def write_out(corrected, images, corrected_out, images_out, sem):
+    copies = [
+        pltpu.make_async_copy(corrected, corrected_out, sem.at[0]),
+        pltpu.make_async_copy(images, images_out, sem.at[1]),
+    ]
+    for copy in copies:
+        copy.start()
+    for copy in copies:
+        copy.wait()
 
 
 def local(sizes, phase_field, thermal, velocity, transfer_slope, transfer_offset, transfer_gain):
@@ -630,6 +644,17 @@
             )
         )
     )
+    corrected, images = pl.pallas_call(
+        write_out,
+        out_shape=(
+            jax.ShapeDtypeStruct((3 * R, Y), f32),
+            jax.ShapeDtypeStruct((4 * X, Y), f32),
+        ),
+        in_specs=[vmem, vmem],
+        out_specs=(hbm, hbm),
+        scratch_shapes=[pltpu.SemaphoreType.DMA((2,))],
+        compiler_params=pltpu.CompilerParams(vmem_limit_bytes=2 * 2**20),
+    )(corrected, images)
     return corrected.reshape(3, Z, X, Y), images.reshape(1, 4, X, Y)
 
 

time: 43.1 us -> 42.2 us (0.979)
  local copies, waits for them, and re-layouts: 1.29 us -> 0 us
    unnamed x2 -> x0, local copies, waits for them, and re-layouts: 1.29 us -> none
    pallas_call x0 -> x1, Pallas kernels: none -> 0.7 us  [local(): pl.pallas_call(write_out, out_shape=(jax.ShapeDtypeStruct((3 * R, Y), f32...]
where the time goes in v5:
time: 42.2 us; the launch traced here: 42.1 us
  Pallas kernels  41.5 us (98%)
  between operations  0.64 us (2%)
    pallas_call x1, Pallas kernels, local(): pl.pallas_call(functools.partial(kernel, sizes), out_shape=(jax.ShapeDtyp...  40.8 us

profile of v5, /device:TPU:8, one launch (start us, length us, event | category | flops | bytes accessed | tf_op | source)
XLA Modules:
  0.0 42.1 jit_solution(10203084336052878561)
XLA Ops:
  0.6 40.8 %shard_map.77 = (f32[384,128]{1,0:T(8,128)S(1)}, f32[64,128]{1,0:T(8,128)S(1)}) custom-call(s32[128,128]{1,0:T(8,128)} %bitcast.8, f32[128,128]{1,0:T(8,128)} %bitcast.9, f32[384,128]{1,0:T(8,128)} %bitcast.7, f32[4,8]{1,0:T(4,128)} %bitcast.10, f32[4,8]{1,0:T(4,128)} %bitcast.11, f32[8]{0:T(128)} %gain_in.1), custom_call_target="tpu_custom_call" | custom-call | tf_op jit(solution)/shard_map/pallas_call | solution.py:579
  41.4 0.7 %shard_map.78 = (f32[384,128]{1,0:T(8,128)}, f32[64,128]{1,0:T(8,128)}) custom-call(f32[384,128]{1,0:T(8,128)S(1)} %get-tuple-element.6.corrected, f32[64,128]{1,0:T(8,128)S(1)} %get-tuple-element.7.images), custom_call_target="tpu_custom_call" | custom-call | tf_op jit(solution)/shard_map/pallas_call | solution.py:647

commit v6 on v5

--- a/solution.py
+++ b/solution.py
@@ -415,12 +415,14 @@
             exchange(p, own, v, inner + rest)
             earlier = late
             if j:
-                fold(last[0] * last[4])
+                step_v = last[0] - v
+                fold(last[5] * step_v)
+                fold(last[4] * step_v)
                 gradient(*earlier)
                 gradient(1, *last[:4])
                 scatter([vel_sum, grads.at[0, 3], grads.at[1, 3]], send_a, recv_a, 8, FAR_FIRST)
-            fold(scaled * v)
             if j == 0:
+                fold(scaled * v)
                 if wide:
                     pl.semaphore_wait(known.at[0], 4)
                 pl.semaphore_wait(known.at[2], 2)
@@ -437,24 +439,26 @@
                 hello(1, 0, 4)
             z_faces, x_faces, both = received(p)
         else:
-            fold(scaled * v)
+            step_v = prior[0] - v
+            fold(prior[1] * step_v)
+            fold(scaled * step_v)
             z_faces, x_faces, both = following
         z_low = jnp.concatenate([edge_z[0:X] * z_faces[0], z_low], axis=0)
         x_edge = coef[8] * spread(x_faces[0], x_faces[-1])
         y_edge = coef[9] * unpack(both)
         x_low = x_low + jnp.where(in_x == 0, x_edge, 0.0)
         y_low = y_low + jnp.where(lane == 0, y_edge, 0.0)
+        prior = (v, scaled)
         if j < 3:
             z_up = jnp.concatenate([z_up, edge_z[X : 2 * X] * z_faces[1]], axis=0)
             scaled = ((z_low + z_up) + rest) + (x_edge + y_edge)
         if j % 2 == 0:
             following = computed(p, v)
-            fold(v * scaled)
             late = (j, v, z_low, x_low, y_low)
         elif j == 1:
-            last = (v, z_low, x_low, y_low, scaled)
+            last = (v, z_low, x_low, y_low, scaled, prior[1])
         else:
-            fold((2.0 * v) * ((z_low + x_low) + y_low))
+            fold(v * (scaled - 2.0 * ((z_low + x_low) + y_low)))
 
     line = jnp.sum(folded[-1], axis=0, keepdims=True)
     row_send[0] = line
@@ -482,11 +486,14 @@
     lane1 = lanes((1, Y))
     m = [jnp.sum(jnp.where(lane1 // 16 == i, line, 0.0), axis=1, keepdims=True) for i in range(8)]
 
-    a = [[m[i + j] - m[i + j + 1] for j in range(4)] for i in range(4)]
-    b = [m[i] for i in range(4)]
+    drop = m[1:]
+    a = [[drop[i + j] for j in range(4)] for i in range(4)]
+    b = [m[0]]
+    for i in range(3):
+        b.append(b[i] - drop[i])
     pivots = []
     for p in range(4):
-        ok = a[p][p] > 1e-7 * (m[2 * p] - m[2 * p + 1])
+        ok = a[p][p] > 1e-7 * drop[2 * p]
         pivots.append(jnp.where(ok, 1.0 / jnp.where(ok, a[p][p], 1.0), 0.0))
         for i in range(p + 1, 4):
             factor = a[p][i] * pivots[p]
@@ -546,19 +553,19 @@
         for j in range(4):
             value = value - c[j] * grads[j, d]
         corrected[d * R : (d + 1) * R] = value
-    whole(img_recv.at[pl.ds(0, 8 * (nz - 1))], 11).wait_recv()
-    for i in range(4):
-        for r in range(2):
-            images[i * X + 8 * r : i * X + 8 * r + 8] = img_recv[pl.ds(2 * i + r, 8, stride=8)]
-
     whole(h1, 0).wait_send()
     whole(stat, 3).wait_send()
     for p in range(2):
         whole(h.at[p, waits[p]], 1 + p).wait_send()
     whole(row_plane.at[pl.ds(0, len(others))], 5).wait_send()
     whole(row_line.at[pl.ds(0, nz - 1)], 6).wait_send()
-    for ref, group_id in ((recv_a, 8), (recv_c, 10), (img_recv, 11)):
+    for ref, group_id in ((recv_a, 8), (recv_c, 10)):
         whole(ref.at[pl.ds(0, ref.shape[0] // nz * (nz - 1))], group_id).wait_send()
+    whole(img_recv.at[pl.ds(0, 8 * (nz - 1))], 11).wait_recv()
+    whole(img_recv.at[pl.ds(0, 8 * (nz - 1))], 11).wait_send()
+    for i in range(4):
+        for r in range(2):
+            images[i * X + 8 * r : i * X + 8 * r + 8] = img_recv[pl.ds(2 * i + r, 8, stride=8)]
 
 
 def write_out(corrected, images, corrected_out, images_out, sem):

time: 42.2 us -> 42.2 us (level)
  no operation moved by 1% of the time
where the time goes in v6:
time: 42.2 us; the launch traced here: 42.1 us
  Pallas kernels  41.5 us (98%)
  between operations  0.64 us (2%)
    pallas_call x1, Pallas kernels, local(): pl.pallas_call(functools.partial(kernel, sizes), out_shape=(jax.ShapeDtyp...  40.8 us

profile of v6, /device:TPU:8, one launch (start us, length us, event | category | flops | bytes accessed | tf_op | source)
XLA Modules:
  0.0 42.1 jit_solution(1838719820154996414)
XLA Ops:
  0.6 40.8 %shard_map.77 = (f32[384,128]{1,0:T(8,128)S(1)}, f32[64,128]{1,0:T(8,128)S(1)}) custom-call(s32[128,128]{1,0:T(8,128)} %bitcast.8, f32[128,128]{1,0:T(8,128)} %bitcast.9, f32[384,128]{1,0:T(8,128)} %bitcast.7, f32[4,8]{1,0:T(4,128)} %bitcast.10, f32[4,8]{1,0:T(4,128)} %bitcast.11, f32[8]{0:T(128)} %gain_in.1), custom_call_target="tpu_custom_call" | custom-call | tf_op jit(solution)/shard_map/pallas_call | solution.py:586
  41.4 0.7 %shard_map.78 = (f32[384,128]{1,0:T(8,128)}, f32[64,128]{1,0:T(8,128)}) custom-call(f32[384,128]{1,0:T(8,128)S(1)} %get-tuple-element.6.corrected, f32[64,128]{1,0:T(8,128)S(1)} %get-tuple-element.7.images), custom_call_target="tpu_custom_call" | custom-call | tf_op jit(solution)/shard_map/pallas_call | solution.py:654

commit v7 on v6

--- a/solution.py
+++ b/solution.py
@@ -126,7 +126,11 @@
     loads = [
         pltpu.make_async_copy(phase_in, phase_v, in_sem.at[0]),
         pltpu.make_async_copy(thermal_in, thermal_v, in_sem.at[1]),
-        pltpu.make_async_copy(vel_in, vel_v, in_sem.at[2]),
+    ] + [
+        pltpu.make_async_copy(
+            vel_in.at[pl.ds(d * R, R)], vel_v.at[pl.ds(d * R, R)], in_sem.at[6 + d]
+        )
+        for d in range(3)
     ]
     params = [
         pltpu.make_async_copy(slope_in, slope, in_sem.at[3]),
@@ -168,18 +172,20 @@
     row = lax.broadcasted_iota(jnp.int32, (R, Y), 0)
     in_x = row % X
 
-    for copy in loads:
+    for copy in loads[:2]:
         copy.wait()
     den = (1.0 + 9.0 * phase_v[...].astype(jnp.float32)) * thermal_v[...]
     den_pad[PAD : PAD + R] = den
+    s1xu[...] = den_pad[pl.ds(PAD + X - 1, 8, stride=X)]
+    ends = pack_ends(den)
+    for copy in loads[2:]:
+        copy.wait()
     vel0, vel1, vel2 = vel_v[0:R], vel_v[R : 2 * R], vel_v[2 * R : 3 * R]
     vel1_pad[PAD : PAD + R] = vel1
     s1z[0:X] = den[0:X]
     s1z[X : 2 * X] = vel0[0:X]
     s1x[0:8] = den_pad[pl.ds(PAD, 8, stride=X)]
     s1x[8:16] = vel1_pad[pl.ds(PAD, 8, stride=X)]
-    s1xu[...] = den_pad[pl.ds(PAD + X - 1, 8, stride=X)]
-    ends = pack_ends(den)
     lane8 = lanes((8, Y))
     for k in range(K):
         ends = jnp.where(lane8 == 2 * K + k, pltpu.roll(group(vel2, k), 2 * K + k, 1), ends)
@@ -214,7 +220,8 @@
     by = unpack(merge(h1[72:80], h1[80:88]))
     yb = jnp.where(lane == 0, face(y_first, den, by), pltpu.roll(den, 1, 1))
     ya = jnp.where(lane == Y - 1, face(y_last, den, by), pltpu.roll(den, Y - 1, 1))
-    low_z, up_z = 2.0 * recip(den + zb), 2.0 * recip(den + za)
+    low_z = 2.0 * recip(den + zb)
+    up_z = jnp.concatenate([low_z[X:], 2.0 * recip(den[R - X :] + za[R - X :])], axis=0)
     low_x, up_x = 2.0 * recip(den + xb), 2.0 * recip(den + xa)
     low_y, up_y = 2.0 * recip(den + yb), 2.0 * recip(den + ya)
     inverse = recip(low_z + up_z + low_x + up_x + low_y + up_y)
@@ -325,16 +332,16 @@
             dx[p, side, 16:24] = q
         signs = ((-1, -1), (-1, 1), (1, -1), (1, 1))[: edges[p]]
         for i, (a, b) in enumerate(signs):
-            row_at = PAD + (R - X if a < 0 else 0) + (X - 1 if b < 0 else 0)
-            to = near("gz", iz, nz, a) | near("gx", ix, nx, b)
-            send(own.at[pl.ds(row_at, 1)], hp.at[pl.ds(224 + i, 1)], 1 + p, to)
-        for i, (a, b) in enumerate(signs):
             to = near("gz", iz, nz, a) | near("gy", iy, ny, b)
             send(dy.at[p, pl.ds(0, 8)], hp.at[pl.ds(128 + 8 * i, 8)], 1 + p, to)
         for i, (a, b) in enumerate(signs):
             to = near("gx", ix, nx, a) | near("gy", iy, ny, b)
             side = 1 if a < 0 else 0
             send(dx.at[p, side, pl.ds(8, 16)], hp.at[pl.ds(160 + 16 * i, 16)], 1 + p, to)
+        for i, (a, b) in enumerate(signs):
+            row_at = PAD + (R - X if a < 0 else 0) + (X - 1 if b < 0 else 0)
+            to = near("gz", iz, nz, a) | near("gx", ix, nx, b)
+            send(own.at[pl.ds(row_at, 1)], hp.at[pl.ds(224 + i, 1)], 1 + p, to)
         send(dz.at[p, 1], hp.at[pl.ds(0, 32)], 1 + p, zp)
         send(dz.at[p, 0], hp.at[pl.ds(32, 32)], 1 + p, zm)
         send(dy.at[p], hp.at[pl.ds(96, 16)], 1 + p, yp)
@@ -630,7 +637,7 @@
             pltpu.VMEM((R, Y), f32),
             pltpu.VMEM((TF, 8, Y), f32),
             pltpu.VMEM((TF * 8, Y), f32),
-            pltpu.SemaphoreType.DMA((6,)),
+            pltpu.SemaphoreType.DMA((9,)),
             pltpu.SemaphoreType.DMA((12,)),
             pltpu.SemaphoreType.DMA((12,)),
             pltpu.SemaphoreType.REGULAR((3,)),

time: 42.2 us -> 42.3 us (level)
  no operation moved by 1% of the time
where the time goes in v7:
time: 42.3 us; the launch traced here: 42.1 us
  Pallas kernels  41.5 us (98%)
  between operations  0.64 us (2%)
    pallas_call x1, Pallas kernels, local(): pl.pallas_call(functools.partial(kernel, sizes), out_shape=(jax.ShapeDtyp...  40.8 us

profile of v7, /device:TPU:8, one launch (start us, length us, event | category | flops | bytes accessed | tf_op | source)
XLA Modules:
  0.0 42.1 jit_solution(6821523618805190736)
XLA Ops:
  0.6 40.8 %shard_map.77 = (f32[384,128]{1,0:T(8,128)S(1)}, f32[64,128]{1,0:T(8,128)S(1)}) custom-call(s32[128,128]{1,0:T(8,128)} %bitcast.8, f32[128,128]{1,0:T(8,128)} %bitcast.9, f32[384,128]{1,0:T(8,128)} %bitcast.7, f32[4,8]{1,0:T(4,128)} %bitcast.10, f32[4,8]{1,0:T(4,128)} %bitcast.11, f32[8]{0:T(128)} %gain_in.1), custom_call_target="tpu_custom_call" | custom-call | tf_op jit(solution)/shard_map/pallas_call | solution.py:593
  41.4 0.7 %shard_map.78 = (f32[384,128]{1,0:T(8,128)}, f32[64,128]{1,0:T(8,128)}) custom-call(f32[384,128]{1,0:T(8,128)S(1)} %get-tuple-element.6.corrected, f32[64,128]{1,0:T(8,128)S(1)} %get-tuple-element.7.images), custom_call_target="tpu_custom_call" | custom-call | tf_op jit(solution)/shard_map/pallas_call | solution.py:661
